TPU v7x, 256 devices: a whole 4x4x8 slice. The times are simulated.
256 devices in a mesh: seq: 32 (over z, y_lo, core), section: 8 (over y_hi, x).
Axes of the slice: x: 4, y: 4 (y_hi: 2, y_lo: 2; y = y_hi * 2 + y_lo), z: 8, core: 2. Of those that a mesh axis runs over, the one named last changes fastest.
Arguments:
- inputs: bfloat16 [8, 4096, 2048], P('section', 'seq'), may hold values from -6 to 6
- b_proj: bfloat16 [8, 4096, 128], P('section', 'seq'), may hold values from -0.59765625 to 0.59765625
- c_proj: bfloat16 [8, 4096, 128], P('section', 'seq'), may hold values from -0.59765625 to 0.59765625
- decay_log: float32 [8, 4096, 32], P('section', 'seq'), may hold values from -1 to 0, as said below
- level_weight: float32 [8, 4096, 6, 32], P('section', 'seq'), may hold values from 0.25 to 2
- out_grad: bfloat16 [8, 4096, 2048], P('section', 'seq'), may hold values from -6 to 6
- final_state_grad: float32 [8, 32, 128, 64], P('section'), may hold values from -0.125 to 0.125
Outputs:
- upstream_grad: bfloat16 [8, 4096, 2048], P('section', 'seq')
- b_grad: float32 [8, 4096, 128], P('section', 'seq')
- c_grad: float32 [8, 4096, 128], P('section', 'seq')
- decay_grad: float32 [8, 4096, 32], P('section', 'seq')
- weight_grad: float32 [8, 4096, 6, 32], P('section', 'seq')
Inputs may be any that keep to these rules, and one draw needn't show every extreme that they name: `decay_log`: negative; per head a rate that varies from token to token and from block to block.
All inputs are finite; a program needn't handle non-finite values.
Results may differ from a plain program's by a relative error of at most 0.001.
Values may be sent and summed in bfloat16 or wider, within the bound.
A program may use at most 128 MiB of HBM per device.

v0:
```python
from functools import partial

import jax
import jax.numpy as jnp
from jax import lax
from jax.sharding import PartitionSpec as P

highest = lax.Precision.HIGHEST


def from_partner(value, axis, apart):
    return lax.ppermute(value, axis, [(i, i ^ 1 << apart) for i in range(lax.axis_size(axis))])


def passed_along(block, axis, distance):
    devices = range(lax.axis_size(axis))
    route = [((i - distance) % len(devices), i) for i in devices]
    return lax.ppermute(block, axis, route)


def block_state(inputs, b_proj, decay_log):
    length, head_count = decay_log.shape
    running = jnp.cumsum(decay_log, axis=0)
    block_total = running[-1]
    factor = jnp.exp(block_total[None, :] - running)
    weighted = inputs.astype(jnp.float32).reshape(length, head_count, -1) * factor[:, :, None]
    state = jnp.einsum("tn,thp->hnp", b_proj.astype(jnp.float32), weighted, precision=highest)
    return (state, block_total)


def block_mixer(inputs, b_proj, c_proj, decay_log, level_weight, carries):
    length, head_count = decay_log.shape
    running = jnp.cumsum(decay_log, axis=0)
    values = inputs.reshape(length, head_count, -1)
    scores = jnp.dot(c_proj, b_proj.T, precision=highest)
    causal = jnp.arange(length)[:, None] >= jnp.arange(length)[None, :]
    spread = running[:, None, :] - running[None, :, :]
    decays = jnp.exp(jnp.where(causal[:, :, None], spread, -jnp.inf))
    mixing = decays * scores[:, :, None]
    local_part = jnp.einsum("tsh,shp->thp", mixing, values, precision=highest)
    result = level_weight[:, 0, :, None] * local_part
    lift = jnp.exp(running)
    for level_index in range(carries.shape[0]):
        reach = jnp.einsum("tn,hnp->thp", c_proj, carries[level_index], precision=highest)
        result = result + (level_weight[:, level_index + 1, :] * lift)[:, :, None] * reach
    return result.reshape(length, -1)


def merge_level(own_state, own_log, prefix_log, peer_state, peer_log, upper):
    carry = jnp.where(upper, jnp.exp(prefix_log)[:, None, None] * peer_state, 0.0)
    joined = jnp.where(
        upper,
        jnp.exp(own_log)[:, None, None] * peer_state + own_state,
        jnp.exp(peer_log)[:, None, None] * own_state + peer_state,
    )
    new_prefix = jnp.where(upper, prefix_log + peer_log, prefix_log)
    return (carry, joined, own_log + peer_log, new_prefix)


def state_spread(b_proj, decay_log, state_grad):
    running = jnp.cumsum(decay_log, axis=0)
    factor = jnp.exp(running[-1][None, :] - running)
    pulled = jnp.einsum("tn,hnp->thp", b_proj.astype(jnp.float32), state_grad, precision=highest)
    return (factor, pulled)


def state_backward(inputs, decay_log, state_grad, total_grad, factor, pulled):
    length, head_count = decay_log.shape
    values = inputs.astype(jnp.float32).reshape(length, head_count, -1)
    weighted = values * factor[:, :, None]
    b_grad = jnp.einsum("thp,hnp->tn", weighted, state_grad, precision=highest)
    log_grad = jnp.sum(values * pulled, axis=2) * factor
    running_grad = (-log_grad).at[-1].add(total_grad + jnp.sum(log_grad, axis=0))
    decay_grad = jnp.cumsum(running_grad[::-1], axis=0)[::-1]
    return (b_grad, decay_grad)


def body(inputs, b_proj, c_proj, decay_log, level_weight, out_grad, final_state_grad):
    own_inputs = inputs[0]
    own_b = b_proj[0]
    own_c = c_proj[0]
    own_decay = decay_log[0]
    own_weight = level_weight[0]
    own_grad = out_grad[0]
    length, head_count = own_decay.shape
    head_size = own_inputs.shape[1] // head_count
    group = 8
    group_width = group * head_size
    levels = lax.axis_size("seq").bit_length() - 1
    position = lax.axis_index("seq")
    state_now, log_now = block_state(own_inputs, own_b, own_decay)
    prefix_now = jnp.zeros_like(log_now)
    saved = []
    carries = []
    for level_index in range(levels):
        upper = position // 2**level_index % 2 == 1
        peer_state, peer_log = from_partner((state_now, log_now), "seq", level_index)
        saved.append((state_now, log_now, prefix_now, peer_state, peer_log, upper))
        carry_now, state_now, log_now, prefix_now = merge_level(
            state_now, log_now, prefix_now, peer_state, peer_log, upper
        )
        carries.append(carry_now)
    all_carries = jnp.stack(carries)
    b_full = own_b.astype(jnp.float32)
    c_full = own_c.astype(jnp.float32)

    def group_step(group_index, buffers):
        input_buf, b_acc, c_acc, decay_buf, weight_buf, carry_buf = buffers
        first_head = group_index * group
        first_col = group_index * group_width
        piece_inputs = lax.dynamic_slice_in_dim(own_inputs, first_col, group_width, 1).astype(
            jnp.float32
        )
        piece_decay = lax.dynamic_slice_in_dim(own_decay, first_head, group, 1)
        piece_weight = lax.dynamic_slice_in_dim(own_weight, first_head, group, 2)
        piece_carry = lax.dynamic_slice_in_dim(all_carries, first_head, group, 1)
        piece_grad = lax.dynamic_slice_in_dim(own_grad, first_col, group_width, 1).astype(
            jnp.float32
        )
        unused, pull = jax.vjp(
            block_mixer, piece_inputs, b_full, c_full, piece_decay, piece_weight, piece_carry
        )
        grads = pull(piece_grad)
        input_buf = lax.dynamic_update_slice_in_dim(input_buf, grads[0], first_col, 1)
        decay_buf = lax.dynamic_update_slice_in_dim(decay_buf, grads[3], first_head, 1)
        weight_buf = lax.dynamic_update_slice_in_dim(weight_buf, grads[4], first_head, 2)
        carry_buf = lax.dynamic_update_slice_in_dim(carry_buf, grads[5], first_head, 1)
        return (input_buf, b_acc + grads[1], c_acc + grads[2], decay_buf, weight_buf, carry_buf)

    start_buffers = (
        jnp.zeros(own_inputs.shape, jnp.float32),
        jnp.zeros(own_b.shape, jnp.float32),
        jnp.zeros(own_c.shape, jnp.float32),
        jnp.zeros(own_decay.shape, jnp.float32),
        jnp.zeros(own_weight.shape, jnp.float32),
        jnp.zeros(all_carries.shape, jnp.float32),
    )
    input_buf, b_acc, c_acc, decay_buf, weight_buf, carry_grads = lax.fori_loop(
        0, head_count // group, group_step, start_buffers
    )
    state_grad = jnp.where(position == 0, final_state_grad[0], 0.0)
    log_grad = jnp.zeros_like(log_now)
    prefix_grad = jnp.zeros_like(log_now)
    for level_index in reversed(range(levels)):
        own_state, own_log, prefix_log, peer_state, peer_log, upper = saved[level_index]
        unused, pull = jax.vjp(
            partial(merge_level, upper=upper), own_state, own_log, prefix_log, peer_state, peer_log
        )
        own_sg, own_lg, prefix_grad, peer_sg, peer_lg = pull(
            (carry_grads[level_index], state_grad, log_grad, prefix_grad)
        )
        back_state, back_log = from_partner((peer_sg, peer_lg), "seq", level_index)
        state_grad = own_sg + back_state
        log_grad = own_lg + back_log
    factor, pulled = state_spread(own_b, own_decay, state_grad)
    b_extra, decay_extra = state_backward(
        own_inputs, own_decay, state_grad, log_grad, factor, pulled
    )
    input_grad = input_buf + (factor[:, :, None] * pulled).reshape(length, -1)
    upstream = passed_along(input_grad.astype(jnp.bfloat16), "section", -1)
    b_grad = b_acc + b_extra
    decay_grad = decay_buf + decay_extra
    return (upstream[None], b_grad[None], c_acc[None], decay_grad[None], weight_buf[None])


def solution(mesh):
    return jax.shard_map(
        body,
        mesh=mesh,
        in_specs=(
            P("section", "seq", None),
            P("section", "seq", None),
            P("section", "seq", None),
            P("section", "seq", None),
            P("section", "seq", None, None),
            P("section", "seq", None),
            P("section", None, None, None),
        ),
        out_specs=(
            P("section", "seq", None),
            P("section", "seq", None),
            P("section", "seq", None),
            P("section", "seq", None),
            P("section", "seq", None, None),
        ),
        check_vma=False,
    )
```

profile of v0, /device:TPU:1, one launch (start us, length us, event | category | flops | bytes accessed | tf_op | source)
XLA Modules:
  0.0 489.4 jit_solution(14907259448109237370)
XLA Ops:
  5.1 3.3 collective-permute-start
  20.5 20.5 %collective-permute-done.2 = f32[32,128,64]{1,2,0:T(8,128)S(1)} collective-permute-done((f32[32,128,64]{1,2,0:T(8,128)S(1)}, f32[32,128,64]{1,2,0:T(8,128)S(1)}, u32[]{:S(2)}, u32[]{:S(2)}) %collective-permute-start.2) | collective-permute-done | bytes 1048608 | tf_op jit(solution)/shard_map/ppermute | solution.py:12
  42.2 19.1 %collective-permute-done.4 = f32[32,128,64]{1,2,0:T(8,128)S(1)} collective-permute-done((f32[32,128,64]{1,2,0:T(8,128)S(1)}, f32[32,128,64]{1,2,0:T(8,128)S(1)}, u32[]{:S(2)}, u32[]{:S(2)}) %collective-permute-start.4) | collective-permute-done | bytes 1048608 | tf_op jit(solution)/shard_map/ppermute | solution.py:12
  68.2 41.7 %collective-permute-done.6 = f32[32,128,64]{1,2,0:T(8,128)} collective-permute-done((f32[32,128,64]{1,2,0:T(8,128)}, f32[32,128,64]{1,2,0:T(8,128)}, u32[]{:S(2)}, u32[]{:S(2)}) %collective-permute-start.6) | collective-permute-done | bytes 1048608 | tf_op jit(solution)/shard_map/ppermute | solution.py:12
  111.7 5.7 %collective-permute-start.8 = (f32[32,128,64]{1,2,0:T(8,128)S(1)}, f32[32,128,64]{1,2,0:T(8,128)S(1)}, u32[]{:S(2)}, u32[]{:S(2)}) collective-permute-start(f32[32,128,64]{1,2,0:T(8,128)S(1)} %add_select_fusion), channel_id=1, source_target_pairs={{0,128},{8,136},{16,144},{24,152},{32,160},{40,168},{48,176},{56,1... | collective-permute-start | bytes 3145736 | tf_op jit(solution)/shard_map/ppermute | solution.py:12
  120.8 2.4 bitcast_dynamic-update-slice_fusion.1
  123.2 38.5 %collective-permute-done.8 = f32[32,128,64]{1,2,0:T(8,128)S(1)} collective-permute-done((f32[32,128,64]{1,2,0:T(8,128)S(1)}, f32[32,128,64]{1,2,0:T(8,128)S(1)}, u32[]{:S(2)}, u32[]{:S(2)}) %collective-permute-start.8) | collective-permute-done | bytes 1048608 | tf_op jit(solution)/shard_map/ppermute | solution.py:12
  165.4 3.0 broadcast_in_dim.225
  168.4 136.1 %while.26 = (s32[]{:T(128)}, f32[128,2048]{1,0:T(8,128)}, f32[128,128]{1,0:T(8,128)S(1)}, f32[128,128]{1,0:T(8,128)}, f32[128,32]{1,0:T(8,128)}, /*index=5*/f32[...) while((s32[]{:T(128)}, f32[128,2048]{1,0:T(8,128)}, ...), condition=%wide.region_13.14_spmd.clone, body=%wide.region_1.13_spmd.clone.sunk | while | flops 1867705344 | bytes 19362560 | solution.py:138
  306.3 2.9 collective-permute-start.10
  309.2 2.7 collective-permute-start.9
  311.9 38.7 %collective-permute-done.9 = f32[32]{0:T(128)S(1)} collective-permute-done((f32[32]{0:T(128)}, f32[32]{0:T(128)S(1)}, u32[]{:S(2)}, u32[]{:S(2)}) %collective-permute-start.9) | collective-permute-done | bytes 160 | tf_op jit(solution)/shard_map/ppermute | solution.py:12
  352.5 35.3 %collective-permute-done.11 = f32[32,128,64]{1,2,0:T(8,128)S(1)} collective-permute-done((f32[32,128,64]{1,2,0:T(8,128)S(1)}, f32[32,128,64]{1,2,0:T(8,128)S(1)}, u32[]{:S(2)}, u32[]{:S(2)}) %collective-permute-start.11) | collective-permute-done | bytes 1048608 | tf_op jit(solution)/shard_map/ppermute | solution.py:12
  387.9 3.7 fusion.79
  392.0 3.1 collective-permute-start.12
  395.2 23.1 %collective-permute-done.12 = f32[32,128,64]{1,2,0:T(8,128)S(1)} collective-permute-done((f32[32,128,64]{1,2,0:T(8,128)S(1)}, f32[32,128,64]{1,2,0:T(8,128)S(1)}, u32[]{:S(2)}, u32[]{:S(2)}) %collective-permute-start.12) | collective-permute-done | bytes 1048608 | tf_op jit(solution)/shard_map/ppermute | solution.py:12
  420.7 22.3 %collective-permute-done.13 = f32[32,128,64]{1,2,0:T(8,128)S(1)} collective-permute-done((f32[32,128,64]{1,2,0:T(8,128)S(1)}, f32[32,128,64]{1,2,0:T(8,128)S(1)}, u32[]{:S(2)}, u32[]{:S(2)}) %collective-permute-start.13) | collective-permute-done | bytes 1048608 | tf_op jit(solution)/shard_map/ppermute | solution.py:12
  446.1 5.3 %collective-permute-start.16 = (f32[32]{0:T(128)S(1)}, f32[32]{0:T(128)S(1)}, u32[]{:S(2)}, u32[]{:S(2)}) collective-permute-start(f32[32]{0:T(128)S(1)} %exponential_multiply_fusion), channel_id=1, source_target_pairs={{0,128},{8,136},{16,144},{24,152},{32,160},{40,168},{48,176},{56,1... | collective-permute-start | bytes 392 | tf_op jit(solution)/shard_map/ppermute | solution.py:12
  452.5 3.2 collective-permute-start.17
  461.7 4.5 collective-permute-start.20
  468.3 2.5 copy.79
  472.2 5.2 %collective-permute-start.15 = (bf16[128,2048]{1,0:T(8,128)(2,1)S(1)}, bf16[128,2048]{1,0:T(8,128)(2,1)S(1)}, u32[]{:S(2)}, u32[]{:S(2)}) collective-permute-start(bf16[128,2048]{1,0:T(8,128)(2,1)S(1)} %add_convert_fusion), channel_id=1, source_target_pairs={{1,0},{2,1},{3,2},{4,3},{5,4},{6,5},{7,6},{0,7},{9,8},{10,9},{11,1... | collective-permute-start | bytes 1572872 | tf_op jit(solution)/shard_map/ppermute | solution.py:18
  478.5 4.2 fusion.77
  482.7 6.0 %collective-permute-done.15 = bf16[128,2048]{1,0:T(8,128)(2,1)S(1)} collective-permute-done((bf16[128,2048]{1,0:T(8,128)(2,1)S(1)}, bf16[128,2048]{1,0:T(8,128)(2,1)S(1)}, u32[]{:S(2)}, u32[]{:S(2)}) %collective-permute-start.15) | collective-permute-done | bytes 524320 | tf_op jit(solution)/shard_map/ppermute | solution.py:18
  (491 shorter events, 189.9 us)
Async XLA Ops:
  5.1 14.7 %collective-permute-start = (f32[32,128,64]{1,2,0:T(8,128)S(1)}, f32[32,128,64]{1,2,0:T(8,128)S(1)}, u32[]{:S(2)}, u32[]{:S(2)}) collective-permute-start(f32[32,128,64]{1,2,0:T(8,128)S(1)} %convolution_bitcast_fusion.18), channel_id=1, source_target_pairs={{0,8},{8,0},{16,24},{24,16},{32,40},{40,32},{48,56},{56,48},{64,72... | collective-permute-start | bytes 3145736 | tf_op jit(solution)/shard_map/ppermute | solution.py:12
  8.4 2.3 collective-permute-start.1
  10.7 2.5 collective-permute-start.3
  13.2 2.5 collective-permute-start.5
  15.7 3.4 collective-permute-start.7
  19.7 98.7 %copy-start.66 = (f32[32]{0:T(128)}, f32[32]{0:T(128)S(1)}, u32[]{:S(2)}) copy-start(f32[32]{0:T(128)S(1)} %get-tuple-element.482) | copy-start | bytes 388
  19.7 142.0 %copy-start.34 = (f32[32]{0:T(128)}, f32[32]{0:T(128)S(1)}, u32[]{:S(2)}) copy-start(f32[32]{0:T(128)S(1)} %get-tuple-element.477) | copy-start | bytes 388
  19.8 148.6 %copy-start.3 = (f32[32,128,64]{1,2,0:T(8,128)}, f32[32,128,64]{1,2,0:T(8,128)S(1)}, u32[]{:S(2)}) copy-start(f32[32,128,64]{1,2,0:T(8,128)S(1)} %collective-permute-done) | copy-start | bytes 3145732
  20.1 20.9 %collective-permute-start.2 = (f32[32,128,64]{1,2,0:T(8,128)S(1)}, f32[32,128,64]{1,2,0:T(8,128)S(1)}, u32[]{:S(2)}, u32[]{:S(2)}) collective-permute-start(f32[32,128,64]{1,2,0:T(8,128)S(1)} %add_select_fusion.3), channel_id=1, source_target_pairs={{0,16},{8,24},{16,0},{24,8},{32,48},{40,56},{48,32},{56,40},{64,80... | collective-permute-start | bytes 3145736 | tf_op jit(solution)/shard_map/ppermute | solution.py:12
  41.3 20.0 %collective-permute-start.4 = (f32[32,128,64]{1,2,0:T(8,128)S(1)}, f32[32,128,64]{1,2,0:T(8,128)S(1)}, u32[]{:S(2)}, u32[]{:S(2)}) collective-permute-start(f32[32,128,64]{1,2,0:T(8,128)S(1)} %add_select_fusion.2), channel_id=1, source_target_pairs={{0,32},{8,40},{16,48},{24,56},{32,0},{40,8},{48,16},{56,24},{64,96... | collective-permute-start | bytes 3145736 | tf_op jit(solution)/shard_map/ppermute | solution.py:12
  62.6 47.3 %collective-permute-start.6 = (f32[32,128,64]{1,2,0:T(8,128)}, f32[32,128,64]{1,2,0:T(8,128)}, u32[]{:S(2)}, u32[]{:S(2)}) collective-permute-start(f32[32,128,64]{1,2,0:T(8,128)} %add_select_fusion.1), channel_id=1, source_target_pairs={{0,64},{8,72},{16,80},{24,88},{32,96},{40,104},{48,112},{56,120},{... | collective-permute-start | bytes 3145736 | tf_op jit(solution)/shard_map/ppermute | solution.py:12
  111.7 50.0 %collective-permute-start.8 = (f32[32,128,64]{1,2,0:T(8,128)S(1)}, f32[32,128,64]{1,2,0:T(8,128)S(1)}, u32[]{:S(2)}, u32[]{:S(2)}) collective-permute-start(f32[32,128,64]{1,2,0:T(8,128)S(1)} %add_select_fusion), channel_id=1, source_target_pairs={{0,128},{8,136},{16,144},{24,152},{32,160},{40,168},{48,176},{56,1... | collective-permute-start | bytes 3145736 | tf_op jit(solution)/shard_map/ppermute | solution.py:12
  306.3 44.4 %collective-permute-start.10 = (f32[32,128,64]{1,2,0:T(8,128)S(1)}, f32[32,128,64]{1,2,0:T(8,128)S(1)}, u32[]{:S(2)}, u32[]{:S(2)}) collective-permute-start(f32[32,128,64]{1,2,0:T(8,128)S(1)} %fusion.84), channel_id=1, source_target_pairs={{0,128},{8,136},{16,144},{24,152},{32,160},{40,168},{48,176},{56,1... | collective-permute-start | bytes 3145736 | tf_op jit(solution)/shard_map/ppermute | solution.py:12
  309.2 41.5 %collective-permute-start.9 = (f32[32]{0:T(128)}, f32[32]{0:T(128)S(1)}, u32[]{:S(2)}, u32[]{:S(2)}) collective-permute-start(f32[32]{0:T(128)} %get-tuple-element.444), channel_id=1, source_target_pairs={{0,128},{8,136},{16,144},{24,152},{32,160},{40,168},{48,176},{56,1... | collective-permute-start | bytes 392 | tf_op jit(solution)/shard_map/ppermute | solution.py:12
  352.4 35.4 %collective-permute-start.11 = (f32[32,128,64]{1,2,0:T(8,128)S(1)}, f32[32,128,64]{1,2,0:T(8,128)S(1)}, u32[]{:S(2)}, u32[]{:S(2)}) collective-permute-start(f32[32,128,64]{1,2,0:T(8,128)S(1)} %get-tuple-element.441), channel_id=1, source_target_pairs={{0,64},{8,72},{16,80},{24,88},{32,96},{40,104},{48,112},{56,120},{... | collective-permute-start | bytes 3145736 | tf_op jit(solution)/shard_map/ppermute | solution.py:12
  392.0 26.2 %collective-permute-start.12 = (f32[32,128,64]{1,2,0:T(8,128)S(1)}, f32[32,128,64]{1,2,0:T(8,128)S(1)}, u32[]{:S(2)}, u32[]{:S(2)}) collective-permute-start(f32[32,128,64]{1,2,0:T(8,128)S(1)} %fusion.80), channel_id=1, source_target_pairs={{0,32},{8,40},{16,48},{24,56},{32,0},{40,8},{48,16},{56,24},{64,96... | collective-permute-start | bytes 3145736 | tf_op jit(solution)/shard_map/ppermute | solution.py:12
  419.4 23.7 %collective-permute-start.13 = (f32[32,128,64]{1,2,0:T(8,128)S(1)}, f32[32,128,64]{1,2,0:T(8,128)S(1)}, u32[]{:S(2)}, u32[]{:S(2)}) collective-permute-start(f32[32,128,64]{1,2,0:T(8,128)S(1)} %fusion.78), channel_id=1, source_target_pairs={{0,16},{8,24},{16,0},{24,8},{32,48},{40,56},{48,32},{56,40},{64,80... | collective-permute-start | bytes 3145736 | tf_op jit(solution)/shard_map/ppermute | solution.py:12
  444.1 22.1 %collective-permute-start.14 = (f32[32,128,64]{1,2,0:T(8,128)S(1)}, f32[32,128,64]{1,2,0:T(8,128)S(1)}, u32[]{:S(2)}, u32[]{:S(2)}) collective-permute-start(f32[32,128,64]{1,2,0:T(8,128)S(1)} %bitcast_add_fusion), channel_id=1, source_target_pairs={{0,8},{8,0},{16,24},{24,16},{32,40},{40,32},{48,56},{56,48},{64,72... | collective-permute-start | bytes 3145736 | tf_op jit(solution)/shard_map/ppermute | solution.py:12
  446.1 6.3 %collective-permute-start.16 = (f32[32]{0:T(128)S(1)}, f32[32]{0:T(128)S(1)}, u32[]{:S(2)}, u32[]{:S(2)}) collective-permute-start(f32[32]{0:T(128)S(1)} %exponential_multiply_fusion), channel_id=1, source_target_pairs={{0,128},{8,136},{16,144},{24,152},{32,160},{40,168},{48,176},{56,1... | collective-permute-start | bytes 392 | tf_op jit(solution)/shard_map/ppermute | solution.py:12
  452.5 4.1 collective-permute-start.17
  456.6 2.5 collective-permute-start.18
  459.2 2.5 collective-permute-start.19
  461.7 15.8 %collective-permute-start.20 = (f32[32]{0:T(128)S(1)}, f32[32]{0:T(128)S(1)}, u32[]{:S(2)}, u32[]{:S(2)}) collective-permute-start(f32[32]{0:T(128)S(1)} %get-tuple-element.429), channel_id=1, source_target_pairs={{0,8},{8,0},{16,24},{24,16},{32,40},{40,32},{48,56},{56,48},{64,72... | collective-permute-start | bytes 392 | tf_op jit(solution)/shard_map/ppermute | solution.py:12
  472.2 16.5 %collective-permute-start.15 = (bf16[128,2048]{1,0:T(8,128)(2,1)S(1)}, bf16[128,2048]{1,0:T(8,128)(2,1)S(1)}, u32[]{:S(2)}, u32[]{:S(2)}) collective-permute-start(bf16[128,2048]{1,0:T(8,128)(2,1)S(1)} %add_convert_fusion), channel_id=1, source_target_pairs={{1,0},{2,1},{3,2},{4,3},{5,4},{6,5},{7,6},{0,7},{9,8},{10,9},{11,1... | collective-permute-start | bytes 1572872 | tf_op jit(solution)/shard_map/ppermute | solution.py:18
  (98 other events, 3147.7 us)
where the time goes:
time: 493 us; the launch traced here: 489 us
  waiting for transfers between devices  258 us (52%)
  matrix products  104 us (21%)
  starting transfers between devices  47.1 us (10%)
  other arithmetic  44.6 us (9%)
  local copies, waits for them, and re-layouts  33.5 us (7%)
    ppermute x20, waiting for transfers between devices, from_partner(): lax.ppermute(value, axis, [(i, i ^ 1 << apart) for i in range(lax.axis_si...  252 us
    dot_general x60, matrix products, block_mixer(): jnp.einsum('tn,hnp->thp', c_proj, carries[level_index], precision=highest)  65.4 us
    ppermute x20, starting transfers between devices, from_partner(): lax.ppermute(value, axis, [(i, i ^ 1 << apart) for i in range(lax.axis_si...  41.9 us
    dot_general x12, matrix products, block_mixer(): local_part = jnp.einsum('tsh,shp->thp', mixing, values, precision=highest)  21.7 us
  transfers between devices with their start and end apart: 21, of which 17 were waited for; matrix products, arithmetic and copies ran while one was open for 4% of the time, Pallas kernels for 0%

commit v1 on v0

v1 whole, which is shorter than its diff:
```python
import jax
import jax.numpy as jnp
from jax import lax
from jax.experimental import pallas as pl
from jax.experimental.pallas import tpu as pltpu
from jax.sharding import PartitionSpec as P

MESH = pl.DeviceIdType.MESH
F32, BF16 = jnp.float32, jnp.bfloat16
BLK = 128
NB = 4
NZ = 8
HEADS = 32
HQ = HEADS // NB
HP = 64
N = 128
TOK = NB * BLK
COLS = HQ * HP
SECTIONS = 8
DEC, LWT, CPR, GRD, BPR, INP = range(6)
TOT, DZK, STA, DST, ZKK, DTT = 0, 1, 4, 5, 6, 9


def level_of(low, high):
    return (low ^ high).bit_length() - 1


def split(value):
    high = value.astype(BF16)
    return high, (value - high.astype(F32)).astype(BF16)


def mm(a, b):
    return jnp.dot(a, b, preferred_element_type=F32)


def mm_split(a, b16):
    high, low = split(a)
    return mm(high, b16) + mm(low, b16)


def lanes_sum(value, tri):
    first = value.astype(BF16)
    rest = value - first.astype(F32)
    second = rest.astype(BF16)
    third = (rest - second.astype(F32)).astype(BF16)
    return mm(first, tri) + mm(second, tri) + mm(third, tri)


def kernel(
    x_hbm, g_hbm, b_hbm, c_hbm, dec_hbm, lw_hbm, fsg_hbm,
    up_out, db_out, dc_out, wg_out, dg_out,
    xa, ga, ba, ca, dec, lw, fsg,
    xt, gt, gt16, bt16, ct16,
    r_rows, e_rows, f_rows, a_rows, w_rows,
    ag, fx, sp, dp, attn, ups,
    dz, st, tot, dzi, sti, dso, zko, dto, dsf, zkf, dti,
    wg, dct, dbs, dcs, dbi, dci, wgs, dgs, xdx,
    a_send, a_recv, z_send, z_recv, u_send, u_recv, o_send, o_recv, loc,
):
    seq = lax.axis_index("seq")
    sec = lax.axis_index("section")
    z = seq // NB
    q = lax.rem(seq, NB)
    before = lax.rem(sec + SECTIONS - 1, SECTIONS)
    after = lax.rem(sec + 1, SECTIONS)

    def at(zz, qq, section=sec):
        return {"seq": zz * NB + qq, "section": section}

    def remote(src, dst, send_sem, recv_sem, where):
        return pltpu.make_async_remote_copy(
            src_ref=src, dst_ref=dst, send_sem=send_sem, recv_sem=recv_sem,
            device_id=where, device_id_type=MESH,
        )

    barrier = pltpu.get_barrier_semaphore()

    def greet(where):
        pl.semaphore_signal(barrier, inc=1, device_id=where, device_id_type=MESH)

    for o in range(1, NB):
        greet(at(z, lax.rem(q + o, NB)))
    for o in range(1, NZ):
        greet(at(lax.rem(z + o, NZ), q))
    for i in range(NB):
        greet(at(z, i, before))
        greet(at(z, i, after))
    pl.semaphore_wait(barrier, NB - 1 + NZ - 1 + 2 * NB)

    def piece(kind, owner, slot):
        heads = pl.ds(pl.multiple_of(owner * HQ, HQ), HQ)
        cols = pl.ds(pl.multiple_of(owner * COLS, COLS), COLS)
        rows = pl.ds(pl.multiple_of(slot * BLK, BLK), BLK)
        if kind == DEC:
            return dec_hbm.at[heads, :], dec.at[slot]
        if kind == LWT:
            return lw_hbm.at[:, heads, :], lw.at[slot]
        if kind == CPR:
            return c_hbm, ca.at[rows, :]
        if kind == GRD:
            return g_hbm.at[:, cols], ga.at[rows, :]
        if kind == BPR:
            return b_hbm, ba.at[rows, :]
        return x_hbm.at[:, cols], xa.at[rows, :]

    def group_send(kind, o):
        peer = lax.rem(q + o, NB)
        src, dst = piece(kind, peer, q)
        return remote(src, dst, a_send.at[kind, o], a_recv.at[kind, q], at(z, peer))

    def group_start(kind):
        for o in range(1, NB):
            group_send(kind, o).start()
        src, dst = piece(kind, q, q)
        pltpu.make_async_copy(src, dst, loc.at[kind]).start()

    def group_wait(kind):
        src, dst = piece(kind, q, q)
        pltpu.make_async_copy(src, dst, loc.at[kind]).wait()
        for o in range(1, NB):
            peer = lax.rem(q + o, NB)
            dst = piece(kind, peer, peer)[1]
            remote(dst, dst, a_send.at[kind, o], a_recv.at[kind, peer], at(z, peer)).wait_recv()

    for kind in (DEC, LWT, CPR, GRD, BPR, INP):
        group_start(kind)
    final_copy = pltpu.make_async_copy(fsg_hbm.at[q * HQ + z], fsg, loc.at[6])
    final_copy.start()

    row_of = lax.broadcasted_iota(jnp.int32, (BLK, BLK), 0)
    col_of = lax.broadcasted_iota(jnp.int32, (BLK, BLK), 1)
    causal = row_of <= col_of
    upto = jnp.where(causal, 1.0, 0.0).astype(BF16)
    onward = jnp.where(row_of >= col_of, 1.0, 0.0).astype(BF16)
    left = lax.broadcasted_iota(jnp.int32, (BLK, BLK), 1) < HP

    group_wait(DEC)
    running = lanes_sum(jnp.concatenate([dec[i] for i in range(NB)], axis=0), upto)
    sofar = jnp.zeros((HQ, 1), F32)
    for i in range(NB):
        own = running[i * HQ : (i + 1) * HQ]
        r_rows[:, i * BLK : (i + 1) * BLK] = own + sofar
        sofar = sofar + own[:, BLK - 1 : BLK]
    tot[z] = jnp.broadcast_to(sofar, (HQ, BLK))

    def z_send_one(kind, o, src, dst, slot_kind=None):
        peer = lax.rem(z + o, NZ)
        return remote(src, dst, z_send.at[kind, o], z_recv.at[kind, z], at(peer, q))

    def z_wait(kind, dst, peer):
        remote(dst, dst, z_send.at[kind, 0], z_recv.at[kind, peer], at(peer, q)).wait_recv()

    @pl.loop(1, NZ)
    def _(o):
        z_send_one(TOT, o, tot.at[z], tot.at[z]).start()

    r_all = r_rows[...]
    e_rows[...] = jnp.exp(r_all)
    f_rows[...] = jnp.exp(sofar - r_all)
    group_wait(LWT)
    for k in range(3):
        for i in range(NB):
            a_rows[k, :, i * BLK : (i + 1) * BLK] = lw[i, 3 + k] * e_rows[:, i * BLK : (i + 1) * BLK]
    for i in range(NB):
        for j in range(i, NB):
            w_rows[i, :, j * BLK : (j + 1) * BLK] = lw[j, level_of(i, j) + 1]

    group_wait(CPR)
    for i in range(NB):
        ct16[:, i * BLK : (i + 1) * BLK] = ca[i * BLK : (i + 1) * BLK, :].astype(F32).T.astype(BF16)
    wg[...] = jnp.zeros_like(wg)
    dct[...] = jnp.zeros_like(dct)
    dp[...] = jnp.zeros_like(dp)

    group_wait(GRD)

    @pl.loop(0, NB)
    def _(c):
        cols = pl.ds(pl.multiple_of(c * BLK, BLK), BLK)
        for i in range(NB):
            rows = ga[i * BLK : (i + 1) * BLK, cols].astype(F32).T
            gt[cols, i * BLK : (i + 1) * BLK] = rows
            gt16[cols, i * BLK : (i + 1) * BLK] = rows.astype(BF16)

    def bit(zz, k):
        return lax.rem(zz // 2**k, 2) == 1

    def head_rows(h):
        return pl.ds(pl.multiple_of(h * HP, HP), HP)

    for k in range(3):

        @pl.when(bit(z, k))
        def _(k=k):
            @pl.loop(0, HQ)
            def _(h):
                high, low = split(gt[head_rows(h), :] * a_rows[k, pl.ds(h, 1), :])
                ag[k, 0, head_rows(h), :] = high
                ag[k, 1, head_rows(h), :] = low

            dz[k] = mm(ag[k, 0], ca[...]) + mm(ag[k, 1], ca[...])
            dzi[k, z] = dz[k, head_rows(z), :]

            @pl.loop(1, NZ)
            def _(o):
                peer = lax.rem(z + o, NZ)
                z_send_one(DZK + k, o, dz.at[k, head_rows(peer), :], dzi.at[k, z]).start()

    group_wait(BPR)
    for i in range(NB):
        bt16[:, i * BLK : (i + 1) * BLK] = ba[i * BLK : (i + 1) * BLK, :].astype(F32).T.astype(BF16)
    group_wait(INP)

    @pl.loop(0, NB)
    def _(c):
        cols = pl.ds(pl.multiple_of(c * BLK, BLK), BLK)
        for i in range(NB):
            xt[cols, i * BLK : (i + 1) * BLK] = xa[i * BLK : (i + 1) * BLK, cols].astype(F32).T

    @pl.loop(0, HQ)
    def _(h):
        high, low = split(xt[head_rows(h), :] * f_rows[pl.ds(h, 1), :])
        fx[0, head_rows(h), :] = high
        fx[1, head_rows(h), :] = low

    st[...] = mm(fx[0], ba[...]) + mm(fx[1], ba[...])
    sti[z] = st[head_rows(z), :]

    @pl.loop(1, NZ)
    def _(o):
        peer = lax.rem(z + o, NZ)
        z_send_one(STA, o, st.at[head_rows(peer), :], sti.at[z]).start()

    sp[...] = mm(ba[...], ct16[...])

    @pl.loop(0, NB)
    def _(p):
        cols = pl.ds(pl.multiple_of(p * BLK, BLK), BLK)
        runs = [r_rows[pl.ds(2 * p + half, 1), :] for half in range(2)]
        found = [{(level, j): jnp.zeros((1, BLK), F32) for level in range(3) for j in range(NB)} for _ in range(2)]
        for i in range(NB):
            keys = slice(i * BLK, (i + 1) * BLK)
            pair = []
            for half in range(2):
                keep = left if half == 0 else jnp.logical_not(left)
                own = jnp.where(keep, xa[keys, cols].astype(F32), 0.0).astype(BF16)
                run = runs[half]
                weights = w_rows[i, pl.ds(2 * p + half, 1), :]
                r_keys = jnp.broadcast_to(run[:, keys], (BLK, BLK)).T
                grad = jnp.zeros((BLK, BLK), F32)
                for j in range(i, NB):
                    queries = slice(j * BLK, (j + 1) * BLK)
                    product = mm(own, gt16[cols, queries])
                    spread = run[:, queries] - r_keys
                    if i == j:
                        spread = jnp.where(causal, spread, -1e30)
                    decay = jnp.exp(spread)
                    score = sp[keys, queries]
                    level = level_of(i, j) + 1
                    found[half][level, j] += jnp.sum(product * decay * score, axis=0, keepdims=True)
                    decay = decay * weights[:, queries]
                    dp[keys, queries] += product * decay
                    grad = grad + mm_split(score * decay, ga[queries, cols])
                pair.append(grad)
            attn[cols, keys] = jnp.where(left, pair[0], pair[1]).T
        for half in range(2):
            for level in range(3):
                row = jnp.concatenate([found[half][level, j] for j in range(NB)], axis=1)
                wg[level, pl.ds(2 * p + half, 1), :] = row

    @pl.loop(1, NZ)
    def _(o):
        peer = lax.rem(z + o, NZ)
        z_wait(TOT, tot.at[peer], peer)

    for k in range(3):

        @pl.loop(1, NZ)
        def _(o, k=k):
            peer = lax.rem(z + o, NZ)

            @pl.when(bit(peer, k))
            def _():
                z_wait(DZK + k, dzi.at[k, peer], peer)

    final_copy.wait()
    totals = [tot[d, pl.ds(z, 1), :] for d in range(NZ)]
    weight = {}
    for e in range(NZ):
        gap = jnp.zeros((1, BLK), F32)
        for d in range(e + 1, NZ):
            weight[e, d] = jnp.exp(gap)
            gap = gap + totals[d]
        weight[e, NZ] = jnp.exp(gap)
    for e in range(NZ):
        grad = weight[e, NZ] * fsg[...]
        for d in range(e + 1, NZ):
            grad = grad + weight[e, d] * dzi[level_of(e, d), d]
        dso[e] = grad

    dsf[head_rows(z), :] = dso[z]

    @pl.loop(1, NZ)
    def _(o):
        peer = lax.rem(z + o, NZ)
        z_send_one(DST, o, dso.at[peer], dsf.at[head_rows(z), :]).start()

    @pl.loop(1, NZ)
    def _(o):
        peer = lax.rem(z + o, NZ)
        z_wait(STA, sti.at[peer], peer)

    for d in range(1, NZ):
        for k in range(3):
            if d >> k & 1:
                base = d - d % 2 ** (k + 1)
                carry = jnp.zeros((HP, N), F32)
                for e in range(base, base + 2**k):
                    carry = carry + weight[e, d] * sti[e]
                zko[k, d] = carry

    for k in range(3):

        @pl.when(bit(z, k))
        def _(k=k):
            zkf[k, head_rows(z), :] = zko[k, z]

        @pl.loop(1, NZ)
        def _(o, k=k):
            peer = lax.rem(z + o, NZ)

            @pl.when(bit(peer, k))
            def _():
                z_send_one(ZKK + k, o, zko.at[k, peer], zkf.at[k, head_rows(z), :]).start()

    def fold(value):
        return sum(value[8 * i : 8 * (i + 1)] for i in range(HP // 8))

    across = [jnp.zeros((8, N), F32) for _ in range(NZ)]
    for e in range(NZ):
        for d in range(e + 1, NZ + 1):
            other = fsg[...] if d == NZ else dzi[level_of(e, d), d]
            shared = weight[e, d] * fold(sti[e] * other)
            for f in range(e, d):
                across[f] = across[f] + shared
    for f in range(NZ):
        dto[f] = across[f]
    dti[z] = dto[z]

    @pl.loop(1, NZ)
    def _(o):
        peer = lax.rem(z + o, NZ)
        z_send_one(DTT, o, dto.at[peer], dti.at[z]).start()

    @pl.loop(1, NZ)
    def _(o):
        peer = lax.rem(z + o, NZ)
        z_wait(DST, dsf.at[head_rows(peer), :], peer)

    @pl.loop(0, NB)
    def _(p):
        cols = pl.ds(pl.multiple_of(p * BLK, BLK), BLK)
        spread = mm_split(dsf[cols, :], bt16[...])
        factor = jnp.concatenate(
            [jnp.broadcast_to(f_rows[pl.ds(2 * p + half, 1), :], (HP, TOK)) for half in range(2)], axis=0
        )
        grad = attn[cols, :] + factor * spread
        own = grad * xt[cols, :]
        for half in range(2):
            xdx[pl.ds(2 * p + half, 1), :] = jnp.sum(own[half * HP : (half + 1) * HP], axis=0, keepdims=True)
        for i in range(NB):
            ups[i * BLK : (i + 1) * BLK, cols] = grad[:, i * BLK : (i + 1) * BLK].T.astype(BF16)

    def up_send(i):
        there = up_out.at[:, pl.ds(pl.multiple_of(q * COLS, COLS), COLS)]
        return remote(ups.at[i * BLK : (i + 1) * BLK, :], there, u_send.at[i], u_recv.at[q], at(z, i, before))

    for i in range(NB):
        up_send(i).start()

    db_t = jnp.zeros((N, TOK), F32)
    high, low = split(jnp.concatenate([dsf[c * BLK : (c + 1) * BLK, :].T for c in range(NB)], axis=1))
    db_t = mm(high, fx[0]) + mm(low, fx[0]) + mm(high, fx[1])
    for i in range(NB):
        keys = slice(i * BLK, (i + 1) * BLK)
        dbs[i] = mm_split(dp[keys, :], ca[...]) + db_t[:, keys].T

    def sum_send(kind, o):
        peer = lax.rem(q + o, NB)
        src, dst = ((dbs, dbi), (dcs, dci))[kind]
        return remote(src.at[peer], dst.at[q], o_send.at[kind, o], o_recv.at[kind, q], at(z, peer))

    for o in range(1, NB):
        sum_send(0, o).start()
    dbi[q] = dbs[q]

    for k in range(3):

        @pl.when(bit(z, k))
        def _(k=k):
            @pl.loop(1, NZ)
            def _(o):
                peer = lax.rem(z + o, NZ)
                z_wait(ZKK + k, zkf.at[k, head_rows(peer), :], peer)

            @pl.loop(0, NB)
            def _(p):
                cols = pl.ds(pl.multiple_of(p * BLK, BLK), BLK)
                reach = mm_split(zkf[k, cols, :], ct16[...]) * gt[cols, :]
                for half in range(2):
                    h = 2 * p + half
                    row = jnp.sum(reach[half * HP : (half + 1) * HP], axis=0, keepdims=True)
                    wg[3 + k, pl.ds(h, 1), :] = row * e_rows[pl.ds(h, 1), :]

            high, low = split(jnp.concatenate([zkf[k, c * BLK : (c + 1) * BLK, :].T for c in range(NB)], axis=1))
            dct[...] += mm(high, ag[k, 0]) + mm(low, ag[k, 0]) + mm(high, ag[k, 1])

    high, low = split(dp[...])
    dc_t = dct[...] + mm(bt16[...], high) + mm(bt16[...], low)
    for i in range(NB):
        dcs[i] = dc_t[:, i * BLK : (i + 1) * BLK].T
    for o in range(1, NB):
        sum_send(1, o).start()
    dci[q] = dcs[q]

    @pl.loop(1, NZ)
    def _(o):
        peer = lax.rem(z + o, NZ)
        z_wait(DTT, dti.at[peer], peer)

    later = jnp.sum(
        jnp.concatenate([jnp.sum(dti[h], axis=0, keepdims=True) for h in range(HQ)], axis=0), axis=1, keepdims=True
    )
    pieces = []
    for i in range(NB):
        here = slice(i * BLK, (i + 1) * BLK)
        change = -xdx[:, here]
        for level in range(6):
            change = change + lw[i, level] * wg[level, :, here]
            wgs[i, level] = wg[level, :, here]
        pieces.append(change)
    sums = lanes_sum(jnp.concatenate(pieces, axis=0), onward)
    for i in reversed(range(NB)):
        own = sums[i * HQ : (i + 1) * HQ]
        dgs[i] = own + later
        later = later + own[:, :1]

    mine = pl.ds(pl.multiple_of(q * HQ, HQ), HQ)

    def rows_send(kind, o):
        peer = lax.rem(q + o, NB)
        src, dst = (wgs.at[peer], wg_out.at[:, mine, :]) if kind == 2 else (dgs.at[peer], dg_out.at[mine, :])
        return remote(src, dst, o_send.at[kind, o], o_recv.at[kind, q], at(z, peer))

    for o in range(1, NB):
        rows_send(2, o).start()
        rows_send(3, o).start()
    own_wg = pltpu.make_async_copy(wgs.at[q], wg_out.at[:, mine, :], loc.at[7])
    own_dg = pltpu.make_async_copy(dgs.at[q], dg_out.at[mine, :], loc.at[8])
    own_wg.start()
    own_dg.start()

    for kind, landed in ((0, dbi), (1, dci)):
        for o in range(1, NB):
            peer = lax.rem(q + o, NB)
            there = landed.at[peer]
            remote(there, there, o_send.at[kind, o], o_recv.at[kind, peer], at(z, peer)).wait_recv()
    db_out[...] = dbi[0] + dbi[1] + dbi[2] + dbi[3]
    dc_out[...] = dci[0] + dci[1] + dci[2] + dci[3]

    own_wg.wait()
    own_dg.wait()
    for o in range(1, NB):
        peer = lax.rem(q + o, NB)
        theirs = pl.ds(pl.multiple_of(peer * HQ, HQ), HQ)
        for kind, there in ((2, wg_out.at[:, theirs, :]), (3, dg_out.at[theirs, :])):
            remote(there, there, o_send.at[kind, o], o_recv.at[kind, peer], at(z, peer)).wait_recv()
    for i in range(NB):
        there = up_out.at[:, i * COLS : (i + 1) * COLS]
        remote(there, there, u_send.at[i], u_recv.at[i], at(z, i, before)).wait_recv()

    for kind in range(6):
        for o in range(1, NB):
            group_send(kind, o).wait_send()
    for i in range(NB):
        up_send(i).wait_send()
    for o in range(1, NB):
        sum_send(0, o).wait_send()
        sum_send(1, o).wait_send()
        rows_send(2, o).wait_send()
        rows_send(3, o).wait_send()

    @pl.loop(1, NZ)
    def _(o):
        peer = lax.rem(z + o, NZ)
        z_send_one(TOT, o, tot.at[z], tot.at[z]).wait_send()
        z_send_one(STA, o, st.at[head_rows(peer), :], sti.at[z]).wait_send()
        z_send_one(DST, o, dso.at[peer], dsf.at[head_rows(z), :]).wait_send()
        z_send_one(DTT, o, dto.at[peer], dti.at[z]).wait_send()
        for k in range(3):

            @pl.when(bit(z, k))
            def _(k=k):
                z_send_one(DZK + k, o, dz.at[k, head_rows(peer), :], dzi.at[k, z]).wait_send()

            @pl.when(bit(peer, k))
            def _(k=k):
                z_send_one(ZKK + k, o, zko.at[k, peer], zkf.at[k, head_rows(z), :]).wait_send()


def body(inputs, b_proj, c_proj, decay_log, level_weight, out_grad, final_state_grad):
    def vmem(*shape, dtype=F32):
        return pltpu.VMEM(shape, dtype)

    scratch = [
        vmem(TOK, COLS, dtype=BF16),
        vmem(TOK, COLS, dtype=BF16),
        vmem(TOK, N, dtype=BF16),
        vmem(TOK, N, dtype=BF16),
        vmem(NB, HQ, BLK),
        vmem(NB, 6, HQ, BLK),
        vmem(HP, N),
        vmem(COLS, TOK),
        vmem(COLS, TOK),
        vmem(COLS, TOK, dtype=BF16),
        vmem(N, TOK, dtype=BF16),
        vmem(N, TOK, dtype=BF16),
        vmem(HQ, TOK),
        vmem(HQ, TOK),
        vmem(HQ, TOK),
        vmem(3, HQ, TOK),
        vmem(NB, HQ, TOK),
        vmem(3, 2, COLS, TOK, dtype=BF16),
        vmem(2, COLS, TOK, dtype=BF16),
        vmem(TOK, TOK),
        vmem(TOK, TOK),
        vmem(COLS, TOK),
        vmem(TOK, COLS, dtype=BF16),
        vmem(3, COLS, N),
        vmem(COLS, N),
        vmem(NZ, HQ, BLK),
        vmem(3, NZ, HP, N),
        vmem(NZ, HP, N),
        vmem(NZ, HP, N),
        vmem(3, NZ, HP, N),
        vmem(NZ, 8, N),
        vmem(COLS, N),
        vmem(3, COLS, N),
        vmem(NZ, 8, N),
        vmem(6, HQ, TOK),
        vmem(N, TOK),
        vmem(NB, BLK, N),
        vmem(NB, BLK, N),
        vmem(NB, BLK, N),
        vmem(NB, BLK, N),
        vmem(NB, 6, HQ, BLK),
        vmem(NB, HQ, BLK),
        vmem(HQ, TOK),
        pltpu.SemaphoreType.DMA((6, NB)),
        pltpu.SemaphoreType.DMA((6, NB)),
        pltpu.SemaphoreType.DMA((10, NZ)),
        pltpu.SemaphoreType.DMA((10, NZ)),
        pltpu.SemaphoreType.DMA((NB,)),
        pltpu.SemaphoreType.DMA((NB,)),
        pltpu.SemaphoreType.DMA((4, NB)),
        pltpu.SemaphoreType.DMA((4, NB)),
        pltpu.SemaphoreType.DMA((9,)),
    ]
    anywhere = pl.BlockSpec(memory_space=pl.ANY)
    near = pl.BlockSpec(memory_space=pltpu.VMEM)
    up, db, dc, wg, dg = pl.pallas_call(
        kernel,
        out_shape=(
            jax.ShapeDtypeStruct((BLK, HEADS * HP), BF16),
            jax.ShapeDtypeStruct((BLK, N), F32),
            jax.ShapeDtypeStruct((BLK, N), F32),
            jax.ShapeDtypeStruct((6, HEADS, BLK), F32),
            jax.ShapeDtypeStruct((HEADS, BLK), F32),
        ),
        in_specs=[anywhere] * 7,
        out_specs=(anywhere, near, near, anywhere, anywhere),
        scratch_shapes=scratch,
        compiler_params=pltpu.CompilerParams(
            collective_id=0, has_side_effects=True, vmem_limit_bytes=40 * 2**20
        ),
    )(
        inputs[0],
        out_grad[0],
        b_proj[0],
        c_proj[0],
        decay_log[0].T,
        jnp.transpose(level_weight[0], (1, 2, 0)),
        jnp.transpose(final_state_grad[0], (0, 2, 1)),
    )
    return (up[None], db[None], dc[None], dg.T[None], jnp.transpose(wg, (2, 0, 1))[None])


def solution(mesh):
    rows = P("section", "seq", None)
    deep = P("section", "seq", None, None)
    return jax.shard_map(
        body,
        mesh=mesh,
        in_specs=(rows, rows, rows, rows, deep, rows, P("section", None, None, None)),
        out_specs=(rows, rows, rows, rows, deep),
        check_vma=False,
    )
```

time: 493 us -> 75 us (0.15)
  the two profiles are of different devices: /device:TPU:1 before, /device:TPU:95 now
where the time goes in v1:
time: 75 us; the launch traced here: 74.5 us
  Pallas kernels  64.1 us (85%)
  local copies, waits for them, and re-layouts  9.72 us (13%)
    pallas_call x1, Pallas kernels, body(): pl.pallas_call(kernel, out_shape=(jax.ShapeDtypeStruct((BLK, HEADS * HP),...  64.1 us
    unnamed x19, local copies, waits for them, and re-layouts  9.72 us

profile of v1, /device:TPU:95, one launch (start us, length us, event | category | flops | bytes accessed | tf_op | source)
XLA Modules:
  0.0 74.5 jit_solution(15721356866207508778)
XLA Ops:
  0.6 0.0 copy-start
  0.6 1.2 %copy-done = f32[1,32,128,64]{2,3,1,0:T(8,128)S(1)} copy-done((f32[1,32,128,64]{2,3,1,0:T(8,128)S(1)}, f32[1,32,128,64]{2,3,1,0:T(8,128)}, u32[]{:S(2)}) %copy-start) | copy-done | bytes 1048600
  1.9 0.0 copy-start.1
  1.9 1.0 %copy-done.1 = bf16[1,128,2048]{2,1,0:T(8,128)(2,1)S(1)} copy-done((bf16[1,128,2048]{2,1,0:T(8,128)(2,1)S(1)}, bf16[1,128,2048]{2,1,0:T(8,128)(2,1)}, u32[]{:S(2)}) %copy-start.1) | copy-done | bytes 524312
  2.9 0.0 copy-start.2
  2.9 1.0 %copy-done.2 = bf16[1,128,2048]{2,1,0:T(8,128)(2,1)S(1)} copy-done((bf16[1,128,2048]{2,1,0:T(8,128)(2,1)S(1)}, bf16[1,128,2048]{2,1,0:T(8,128)(2,1)}, u32[]{:S(2)}) %copy-start.2) | copy-done | bytes 524312
  3.9 0.0 copy-start.3
  3.9 0.9 %copy-done.3 = f32[1,128,6,32]{1,3,2,0:T(8,128)S(1)} copy-done((f32[1,128,6,32]{1,3,2,0:T(8,128)S(1)}, f32[1,128,6,32]{1,3,2,0:T(8,128)}, u32[]{:S(2)}) %copy-start.3) | copy-done | bytes 98328
  4.8 0.0 copy-start.4
  4.8 0.8 %copy-done.4 = bf16[1,128,128]{2,1,0:T(8,128)(2,1)S(1)} copy-done((bf16[1,128,128]{2,1,0:T(8,128)(2,1)S(1)}, bf16[1,128,128]{2,1,0:T(8,128)(2,1)}, u32[]{:S(2)}) %copy-start.4) | copy-done | bytes 32792
  5.6 0.0 copy-start.5
  5.6 0.8 %copy-done.5 = bf16[1,128,128]{2,1,0:T(8,128)(2,1)S(1)} copy-done((bf16[1,128,128]{2,1,0:T(8,128)(2,1)S(1)}, bf16[1,128,128]{2,1,0:T(8,128)(2,1)}, u32[]{:S(2)}) %copy-start.5) | copy-done | bytes 32792
  6.4 0.0 copy-start.6
  6.4 0.7 copy-done.6
  7.1 64.1 %shard_map.110 = (bf16[128,2048]{1,0:T(8,128)(2,1)S(1)}, f32[128,128]{1,0:T(8,128)S(1)}, f32[128,128]{1,0:T(8,128)S(1)}, f32[6,32,128]{2,1,0:T(8,128)S(1)}, f32[32,128]{1,0:T(8,128)S(1)}) custom-call(bf16[128,2048]{1,0:T(8,128)(2,1)S(1)} %bitcast.23, bf16[128,2048]{1,0:T(8,128)(2,1)S(1)} %bitcast.24, bf16[128,128]{1,0:T(8,128)(2,1)S(1)} %bitcast.30, ...), custom_call_target="tpu_custom_call" | custom-call | tf_op jit(solution)/shard_map/pallas_call | solution.py:572
  71.2 0.8 %copy.17 = bf16[1,128,2048]{2,1,0:T(8,128)(2,1)} copy(bf16[1,128,2048]{2,1,0:T(8,128)(2,1)S(1)} %bitcast.25) | data formatting | bytes 1048576
  72.0 0.6 copy.18
  72.6 0.6 copy.19
  73.3 0.6 copy.20
  73.9 0.6 copy.21
Async XLA Ops:
  0.6 1.2 %copy-start = (f32[1,32,128,64]{2,3,1,0:T(8,128)S(1)}, f32[1,32,128,64]{2,3,1,0:T(8,128)}, u32[]{:S(2)}) copy-start(f32[1,32,128,64]{2,3,1,0:T(8,128)} %param.13) | copy-start | bytes 3145732
  1.9 1.0 %copy-start.1 = (bf16[1,128,2048]{2,1,0:T(8,128)(2,1)S(1)}, bf16[1,128,2048]{2,1,0:T(8,128)(2,1)}, u32[]{:S(2)}) copy-start(bf16[1,128,2048]{2,1,0:T(8,128)(2,1)} %param.7) | copy-start | bytes 1572868
  2.9 1.0 %copy-start.2 = (bf16[1,128,2048]{2,1,0:T(8,128)(2,1)S(1)}, bf16[1,128,2048]{2,1,0:T(8,128)(2,1)}, u32[]{:S(2)}) copy-start(bf16[1,128,2048]{2,1,0:T(8,128)(2,1)} %param.12) | copy-start | bytes 1572868
  3.9 0.9 %copy-start.3 = (f32[1,128,6,32]{1,3,2,0:T(8,128)S(1)}, f32[1,128,6,32]{1,3,2,0:T(8,128)}, u32[]{:S(2)}) copy-start(f32[1,128,6,32]{1,3,2,0:T(8,128)} %param.11) | copy-start | bytes 294916
  4.8 0.8 %copy-start.4 = (bf16[1,128,128]{2,1,0:T(8,128)(2,1)S(1)}, bf16[1,128,128]{2,1,0:T(8,128)(2,1)}, u32[]{:S(2)}) copy-start(bf16[1,128,128]{2,1,0:T(8,128)(2,1)} %param.8) | copy-start | bytes 98308
  5.6 0.8 %copy-start.5 = (bf16[1,128,128]{2,1,0:T(8,128)(2,1)S(1)}, bf16[1,128,128]{2,1,0:T(8,128)(2,1)}, u32[]{:S(2)}) copy-start(bf16[1,128,128]{2,1,0:T(8,128)(2,1)} %param.9) | copy-start | bytes 98308
  6.4 0.7 copy-start.6

commit v2 on v1

--- a/solution.py
+++ b/solution.py
@@ -123,7 +123,7 @@
             dst = piece(kind, peer, peer)[1]
             remote(dst, dst, a_send.at[kind, o], a_recv.at[kind, peer], at(z, peer)).wait_recv()
 
-    for kind in (DEC, LWT, CPR, GRD, BPR, INP):
+    for kind in (DEC, LWT, CPR, GRD):
         group_start(kind)
     final_copy = pltpu.make_async_copy(fsg_hbm.at[q * HQ + z], fsg, loc.at[6])
     final_copy.start()
@@ -174,6 +174,8 @@
     dp[...] = jnp.zeros_like(dp)
 
     group_wait(GRD)
+    group_start(BPR)
+    group_start(INP)
 
     @pl.loop(0, NB)
     def _(c):
@@ -568,18 +570,18 @@
         pltpu.SemaphoreType.DMA((9,)),
     ]
     anywhere = pl.BlockSpec(memory_space=pl.ANY)
-    near = pl.BlockSpec(memory_space=pltpu.VMEM)
+    made = (
+        jax.ShapeDtypeStruct((BLK, HEADS * HP), BF16),
+        jax.ShapeDtypeStruct((BLK, N), F32),
+        jax.ShapeDtypeStruct((BLK, N), F32),
+        jax.ShapeDtypeStruct((6, HEADS, BLK), F32),
+        jax.ShapeDtypeStruct((HEADS, BLK), F32),
+    )
     up, db, dc, wg, dg = pl.pallas_call(
         kernel,
-        out_shape=(
-            jax.ShapeDtypeStruct((BLK, HEADS * HP), BF16),
-            jax.ShapeDtypeStruct((BLK, N), F32),
-            jax.ShapeDtypeStruct((BLK, N), F32),
-            jax.ShapeDtypeStruct((6, HEADS, BLK), F32),
-            jax.ShapeDtypeStruct((HEADS, BLK), F32),
-        ),
+        out_shape=made,
         in_specs=[anywhere] * 7,
-        out_specs=(anywhere, near, near, anywhere, anywhere),
+        out_specs=(anywhere, pl.BlockSpec(memory_space=pltpu.VMEM), pl.BlockSpec(memory_space=pltpu.VMEM), anywhere, anywhere),
         scratch_shapes=scratch,
         compiler_params=pltpu.CompilerParams(
             collective_id=0, has_side_effects=True, vmem_limit_bytes=40 * 2**20

time: 75 us -> 76.1 us (1.015)
  Pallas kernels: 64.1 us -> 65.3 us
    pallas_call x1, Pallas kernels: 64.1 us -> 65.3 us  [body(): pl.pallas_call(kernel, out_shape=made, in_specs=[anywhere] * 7, out_specs...]
where the time goes in v2:
time: 76.1 us; the launch traced here: 75.7 us
  Pallas kernels  65.3 us (86%)
  local copies, waits for them, and re-layouts  9.72 us (13%)
    pallas_call x1, Pallas kernels, body(): pl.pallas_call(kernel, out_shape=made, in_specs=[anywhere] * 7, out_specs...  65.3 us
    unnamed x19, local copies, waits for them, and re-layouts  9.72 us

profile of v2, /device:TPU:95, one launch (start us, length us, event | category | flops | bytes accessed | tf_op | source)
XLA Modules:
  0.0 75.7 jit_solution(11382213926027830828)
XLA Ops:
  0.6 0.0 copy-start
  0.6 1.2 %copy-done = f32[1,32,128,64]{2,3,1,0:T(8,128)S(1)} copy-done((f32[1,32,128,64]{2,3,1,0:T(8,128)S(1)}, f32[1,32,128,64]{2,3,1,0:T(8,128)}, u32[]{:S(2)}) %copy-start) | copy-done | bytes 1048600
  1.9 0.0 copy-start.1
  1.9 1.0 %copy-done.1 = bf16[1,128,2048]{2,1,0:T(8,128)(2,1)S(1)} copy-done((bf16[1,128,2048]{2,1,0:T(8,128)(2,1)S(1)}, bf16[1,128,2048]{2,1,0:T(8,128)(2,1)}, u32[]{:S(2)}) %copy-start.1) | copy-done | bytes 524312
  2.9 0.0 copy-start.2
  2.9 1.0 %copy-done.2 = bf16[1,128,2048]{2,1,0:T(8,128)(2,1)S(1)} copy-done((bf16[1,128,2048]{2,1,0:T(8,128)(2,1)S(1)}, bf16[1,128,2048]{2,1,0:T(8,128)(2,1)}, u32[]{:S(2)}) %copy-start.2) | copy-done | bytes 524312
  3.9 0.0 copy-start.3
  3.9 0.9 %copy-done.3 = f32[1,128,6,32]{1,3,2,0:T(8,128)S(1)} copy-done((f32[1,128,6,32]{1,3,2,0:T(8,128)S(1)}, f32[1,128,6,32]{1,3,2,0:T(8,128)}, u32[]{:S(2)}) %copy-start.3) | copy-done | bytes 98328
  4.8 0.0 copy-start.4
  4.8 0.8 copy-done.4
  5.6 0.0 copy-start.5
  5.6 0.8 copy-done.5
  6.4 0.0 copy-start.6
  6.4 0.7 copy-done.6
  7.1 65.3 %shard_map.110 = (bf16[128,2048]{1,0:T(8,128)(2,1)S(1)}, f32[128,128]{1,0:T(8,128)S(1)}, f32[128,128]{1,0:T(8,128)S(1)}, f32[6,32,128]{2,1,0:T(8,128)S(1)}, f32[32,128]{1,0:T(8,128)S(1)}) custom-call(bf16[128,2048]{1,0:T(8,128)(2,1)S(1)} %bitcast.23, bf16[128,2048]{1,0:T(8,128)(2,1)S(1)} %bitcast.24, bf16[128,128]{1,0:T(8,128)(2,1)S(1)} %bitcast.30, ...), custom_call_target="tpu_custom_call" | custom-call | tf_op jit(solution)/shard_map/pallas_call | solution.py:580
  72.4 0.8 %copy.17 = bf16[1,128,2048]{2,1,0:T(8,128)(2,1)} copy(bf16[1,128,2048]{2,1,0:T(8,128)(2,1)S(1)} %bitcast.25) | data formatting | bytes 1048576
  73.2 0.6 copy.18
  73.8 0.6 copy.19
  74.4 0.6 copy.20
  75.0 0.6 copy.21
Async XLA Ops:
  0.6 1.2 %copy-start = (f32[1,32,128,64]{2,3,1,0:T(8,128)S(1)}, f32[1,32,128,64]{2,3,1,0:T(8,128)}, u32[]{:S(2)}) copy-start(f32[1,32,128,64]{2,3,1,0:T(8,128)} %param.13) | copy-start | bytes 3145732
  1.9 1.0 %copy-start.1 = (bf16[1,128,2048]{2,1,0:T(8,128)(2,1)S(1)}, bf16[1,128,2048]{2,1,0:T(8,128)(2,1)}, u32[]{:S(2)}) copy-start(bf16[1,128,2048]{2,1,0:T(8,128)(2,1)} %param.7) | copy-start | bytes 1572868
  2.9 1.0 %copy-start.2 = (bf16[1,128,2048]{2,1,0:T(8,128)(2,1)S(1)}, bf16[1,128,2048]{2,1,0:T(8,128)(2,1)}, u32[]{:S(2)}) copy-start(bf16[1,128,2048]{2,1,0:T(8,128)(2,1)} %param.12) | copy-start | bytes 1572868
  3.9 0.9 %copy-start.3 = (f32[1,128,6,32]{1,3,2,0:T(8,128)S(1)}, f32[1,128,6,32]{1,3,2,0:T(8,128)}, u32[]{:S(2)}) copy-start(f32[1,128,6,32]{1,3,2,0:T(8,128)} %param.11) | copy-start | bytes 294916
  4.8 0.8 %copy-start.4 = (bf16[1,128,128]{2,1,0:T(8,128)(2,1)S(1)}, bf16[1,128,128]{2,1,0:T(8,128)(2,1)}, u32[]{:S(2)}) copy-start(bf16[1,128,128]{2,1,0:T(8,128)(2,1)} %param.8) | copy-start | bytes 98308
  5.6 0.8 %copy-start.5 = (bf16[1,128,128]{2,1,0:T(8,128)(2,1)S(1)}, bf16[1,128,128]{2,1,0:T(8,128)(2,1)}, u32[]{:S(2)}) copy-start(bf16[1,128,128]{2,1,0:T(8,128)(2,1)} %param.9) | copy-start | bytes 98308
  6.4 0.7 copy-start.6

commit v3 on v2

--- a/solution.py
+++ b/solution.py
@@ -17,6 +17,7 @@
 TOK = NB * BLK
 COLS = HQ * HP
 SECTIONS = 8
+AHEAD = 3
 DEC, LWT, CPR, GRD, BPR, INP = range(6)
 TOT, DZK, STA, DST, ZKK, DTT = 0, 1, 4, 5, 6, 9
 
@@ -55,8 +56,8 @@
     r_rows, e_rows, f_rows, a_rows, w_rows,
     ag, fx, sp, dp, attn, ups,
     dz, st, tot, dzi, sti, dso, zko, dto, dsf, zkf, dti,
-    wg, dct, dbs, dcs, dbi, dci, wgs, dgs, xdx,
-    a_send, a_recv, z_send, z_recv, u_send, u_recv, o_send, o_recv, loc,
+    wg, dct, dbs, dcs, dbi, dci, wgs, dgs, xdx, near, low_dz,
+    a_send, a_recv, z_send, z_recv, n_send, n_recv, u_send, u_recv, o_send, o_recv, loc,
 ):
     seq = lax.axis_index("seq")
     sec = lax.axis_index("section")
@@ -88,9 +89,13 @@
         greet(at(z, i, after))
     pl.semaphore_wait(barrier, NB - 1 + NZ - 1 + 2 * NB)
 
-    def piece(kind, owner, slot):
+    def pair_at(j):
+        return lax.rem(z // 2 + 1 + j, NB)
+
+    def piece(kind, owner, slot, j):
         heads = pl.ds(pl.multiple_of(owner * HQ, HQ), HQ)
-        cols = pl.ds(pl.multiple_of(owner * COLS, COLS), COLS)
+        there = pl.ds(pl.multiple_of(pair_at(j) * BLK, BLK), BLK)
+        cols = pl.ds(pl.multiple_of(owner * COLS + pair_at(j) * BLK, BLK), BLK)
         rows = pl.ds(pl.multiple_of(slot * BLK, BLK), BLK)
         if kind == DEC:
             return dec_hbm.at[heads, :], dec.at[slot]
@@ -99,33 +104,35 @@
         if kind == CPR:
             return c_hbm, ca.at[rows, :]
         if kind == GRD:
-            return g_hbm.at[:, cols], ga.at[rows, :]
+            return g_hbm.at[:, cols], ga.at[rows, there]
         if kind == BPR:
             return b_hbm, ba.at[rows, :]
-        return x_hbm.at[:, cols], xa.at[rows, :]
-
-    def group_send(kind, o):
+        return x_hbm.at[:, cols], xa.at[rows, there]
+
+    def group_send(kind, o, j):
         peer = lax.rem(q + o, NB)
-        src, dst = piece(kind, peer, q)
-        return remote(src, dst, a_send.at[kind, o], a_recv.at[kind, q], at(z, peer))
-
-    def group_start(kind):
+        src, dst = piece(kind, peer, q, j)
+        return remote(src, dst, a_send.at[kind, j, o], a_recv.at[kind, j, q], at(z, peer))
+
+    def group_start(kind, j=0):
         for o in range(1, NB):
-            group_send(kind, o).start()
-        src, dst = piece(kind, q, q)
-        pltpu.make_async_copy(src, dst, loc.at[kind]).start()
-
-    def group_wait(kind):
-        src, dst = piece(kind, q, q)
-        pltpu.make_async_copy(src, dst, loc.at[kind]).wait()
+            group_send(kind, o, j).start()
+        src, dst = piece(kind, q, q, j)
+        pltpu.make_async_copy(src, dst, loc.at[kind, j]).start()
+
+    def group_wait(kind, j=0):
+        src, dst = piece(kind, q, q, j)
+        pltpu.make_async_copy(src, dst, loc.at[kind, j]).wait()
         for o in range(1, NB):
             peer = lax.rem(q + o, NB)
-            dst = piece(kind, peer, peer)[1]
-            remote(dst, dst, a_send.at[kind, o], a_recv.at[kind, peer], at(z, peer)).wait_recv()
-
-    for kind in (DEC, LWT, CPR, GRD):
+            dst = piece(kind, peer, peer, j)[1]
+            remote(dst, dst, a_send.at[kind, j, o], a_recv.at[kind, j, peer], at(z, peer)).wait_recv()
+
+    for kind in (DEC, LWT, CPR):
         group_start(kind)
-    final_copy = pltpu.make_async_copy(fsg_hbm.at[q * HQ + z], fsg, loc.at[6])
+    for j in range(AHEAD):
+        group_start(GRD, j)
+    final_copy = pltpu.make_async_copy(fsg_hbm.at[q * HQ + z], fsg, loc.at[6, 0])
     final_copy.start()
 
     row_of = lax.broadcasted_iota(jnp.int32, (BLK, BLK), 0)
@@ -144,16 +151,15 @@
         sofar = sofar + own[:, BLK - 1 : BLK]
     tot[z] = jnp.broadcast_to(sofar, (HQ, BLK))
 
-    def z_send_one(kind, o, src, dst, slot_kind=None):
-        peer = lax.rem(z + o, NZ)
-        return remote(src, dst, z_send.at[kind, o], z_recv.at[kind, z], at(peer, q))
+    def z_send_one(kind, peer, src, dst):
+        return remote(src, dst, z_send.at[kind, peer], z_recv.at[kind, z], at(peer, q))
 
     def z_wait(kind, dst, peer):
         remote(dst, dst, z_send.at[kind, 0], z_recv.at[kind, peer], at(peer, q)).wait_recv()
 
     @pl.loop(1, NZ)
     def _(o):
-        z_send_one(TOT, o, tot.at[z], tot.at[z]).start()
+        z_send_one(TOT, lax.rem(z + o, NZ), tot.at[z], tot.at[z]).start()
 
     r_all = r_rows[...]
     e_rows[...] = jnp.exp(r_all)
@@ -173,66 +179,137 @@
     dct[...] = jnp.zeros_like(dct)
     dp[...] = jnp.zeros_like(dp)
 
-    group_wait(GRD)
-    group_start(BPR)
-    group_start(INP)
+    def bit(zz, k):
+        return lax.rem(zz // 2**k, 2) == 1
+
+    def head_rows(h):
+        return pl.ds(pl.multiple_of(h * HP, HP), HP)
+
+    def pair_rows(p):
+        return pl.ds(pl.multiple_of(p * BLK, BLK), BLK)
+
+    def to_owners(kind, p, source, landing):
+        for half in range(2):
+            owner = 2 * p + half
+
+            @pl.when(owner != z)
+            def _(owner=owner):
+                z_send_one(kind, owner, source.at[head_rows(owner), :], landing.at[z]).start()
+
+            @pl.when(owner == z)
+            def _(owner=owner):
+                landing[z] = source[head_rows(owner), :]
+
+    def down_send(p):
+        return remote(dz.at[0, pair_rows(p), :], low_dz.at[pair_rows(p), :], n_send.at[0, p], n_recv.at[0, p], at(z - 1, q))
+
+    def up_state(p):
+        return remote(st.at[pair_rows(p), :], zkf.at[0, pair_rows(p), :], n_send.at[1, p], n_recv.at[1, p], at(z + 1, q))
 
     @pl.loop(0, NB)
-    def _(c):
-        cols = pl.ds(pl.multiple_of(c * BLK, BLK), BLK)
+    def _(j):
+        p = pair_at(j)
+        cols = pair_rows(p)
+        group_wait(GRD, j)
+
+        @pl.when(j < NB - AHEAD)
+        def _():
+            group_start(GRD, j + AHEAD)
+
+        @pl.when(j == NB - AHEAD)
+        def _():
+            group_start(BPR)
+
+        @pl.when(j >= NB - AHEAD)
+        def _():
+            group_start(INP, j + AHEAD - NB)
+
         for i in range(NB):
             rows = ga[i * BLK : (i + 1) * BLK, cols].astype(F32).T
             gt[cols, i * BLK : (i + 1) * BLK] = rows
             gt16[cols, i * BLK : (i + 1) * BLK] = rows.astype(BF16)
-
-    def bit(zz, k):
-        return lax.rem(zz // 2**k, 2) == 1
-
-    def head_rows(h):
-        return pl.ds(pl.multiple_of(h * HP, HP), HP)
-
-    for k in range(3):
-
-        @pl.when(bit(z, k))
-        def _(k=k):
-            @pl.loop(0, HQ)
-            def _(h):
-                high, low = split(gt[head_rows(h), :] * a_rows[k, pl.ds(h, 1), :])
-                ag[k, 0, head_rows(h), :] = high
-                ag[k, 1, head_rows(h), :] = low
-
-            dz[k] = mm(ag[k, 0], ca[...]) + mm(ag[k, 1], ca[...])
-            dzi[k, z] = dz[k, head_rows(z), :]
-
-            @pl.loop(1, NZ)
-            def _(o):
-                peer = lax.rem(z + o, NZ)
-                z_send_one(DZK + k, o, dz.at[k, head_rows(peer), :], dzi.at[k, z]).start()
+        for k in range(3):
+
+            @pl.when(bit(z, k))
+            def _(k=k):
+                for half in range(2):
+                    rows = head_rows(2 * p + half)
+                    high, low = split(gt[rows, :] * a_rows[k, pl.ds(2 * p + half, 1), :])
+                    ag[k, 0, rows, :] = high
+                    ag[k, 1, rows, :] = low
+                dz[k, cols, :] = mm(ag[k, 0, cols, :], ca[...]) + mm(ag[k, 1, cols, :], ca[...])
+                if k == 0:
+                    down_send(p).start()
+                else:
+                    to_owners(DZK + k, p, dz.at[k], dzi.at[k])
 
     group_wait(BPR)
     for i in range(NB):
         bt16[:, i * BLK : (i + 1) * BLK] = ba[i * BLK : (i + 1) * BLK, :].astype(F32).T.astype(BF16)
-    group_wait(INP)
 
     @pl.loop(0, NB)
-    def _(c):
-        cols = pl.ds(pl.multiple_of(c * BLK, BLK), BLK)
+    def _(j):
+        p = pair_at(j)
+        cols = pair_rows(p)
+        group_wait(INP, j)
+
+        @pl.when(j == 0)
+        def _():
+            group_start(INP, NB - 1)
+
         for i in range(NB):
             xt[cols, i * BLK : (i + 1) * BLK] = xa[i * BLK : (i + 1) * BLK, cols].astype(F32).T
-
-    @pl.loop(0, HQ)
-    def _(h):
-        high, low = split(xt[head_rows(h), :] * f_rows[pl.ds(h, 1), :])
-        fx[0, head_rows(h), :] = high
-        fx[1, head_rows(h), :] = low
-
-    st[...] = mm(fx[0], ba[...]) + mm(fx[1], ba[...])
-    sti[z] = st[head_rows(z), :]
+        for half in range(2):
+            rows = head_rows(2 * p + half)
+            high, low = split(xt[rows, :] * f_rows[pl.ds(2 * p + half, 1), :])
+            fx[0, rows, :] = high
+            fx[1, rows, :] = low
+        st[cols, :] = mm(fx[0, cols, :], ba[...]) + mm(fx[1, cols, :], ba[...])
+
+        @pl.when(jnp.logical_not(bit(z, 0)))
+        def _():
+            up_state(p).start()
+
+        to_owners(STA, p, st, sti)
 
     @pl.loop(1, NZ)
     def _(o):
         peer = lax.rem(z + o, NZ)
-        z_send_one(STA, o, st.at[head_rows(peer), :], sti.at[z]).start()
+        z_wait(TOT, tot.at[peer], peer)
+
+    for k in range(1, 3):
+
+        @pl.loop(1, NZ)
+        def _(o, k=k):
+            peer = lax.rem(z + o, NZ)
+
+            @pl.when(bit(peer, k))
+            def _():
+                z_wait(DZK + k, dzi.at[k, peer], peer)
+
+    final_copy.wait()
+    totals = [tot[d, pl.ds(z, 1), :] for d in range(NZ)]
+    weight = {}
+    for e in range(NZ):
+        gap = jnp.zeros((1, BLK), F32)
+        for d in range(e + 1, NZ):
+            weight[e, d] = jnp.exp(gap)
+            gap = gap + totals[d]
+        weight[e, NZ] = jnp.exp(gap)
+    for e in range(NZ):
+        grad = weight[e, NZ] * fsg[...]
+        for d in range(e + 1, NZ):
+            if level_of(e, d) == 0:
+                continue
+            grad = grad + weight[e, d] * dzi[level_of(e, d), d]
+        dso[e] = grad
+
+    dsf[head_rows(z), :] = dso[z]
+
+    @pl.loop(1, NZ)
+    def _(o):
+        peer = lax.rem(z + o, NZ)
+        z_send_one(DST, peer, dso.at[peer], dsf.at[head_rows(z), :]).start()
 
     sp[...] = mm(ba[...], ct16[...])
 
@@ -274,47 +351,10 @@
     @pl.loop(1, NZ)
     def _(o):
         peer = lax.rem(z + o, NZ)
-        z_wait(TOT, tot.at[peer], peer)
-
-    for k in range(3):
-
-        @pl.loop(1, NZ)
-        def _(o, k=k):
-            peer = lax.rem(z + o, NZ)
-
-            @pl.when(bit(peer, k))
-            def _():
-                z_wait(DZK + k, dzi.at[k, peer], peer)
-
-    final_copy.wait()
-    totals = [tot[d, pl.ds(z, 1), :] for d in range(NZ)]
-    weight = {}
-    for e in range(NZ):
-        gap = jnp.zeros((1, BLK), F32)
-        for d in range(e + 1, NZ):
-            weight[e, d] = jnp.exp(gap)
-            gap = gap + totals[d]
-        weight[e, NZ] = jnp.exp(gap)
-    for e in range(NZ):
-        grad = weight[e, NZ] * fsg[...]
-        for d in range(e + 1, NZ):
-            grad = grad + weight[e, d] * dzi[level_of(e, d), d]
-        dso[e] = grad
-
-    dsf[head_rows(z), :] = dso[z]
-
-    @pl.loop(1, NZ)
-    def _(o):
-        peer = lax.rem(z + o, NZ)
-        z_send_one(DST, o, dso.at[peer], dsf.at[head_rows(z), :]).start()
-
-    @pl.loop(1, NZ)
-    def _(o):
-        peer = lax.rem(z + o, NZ)
         z_wait(STA, sti.at[peer], peer)
 
     for d in range(1, NZ):
-        for k in range(3):
+        for k in range(1, 3):
             if d >> k & 1:
                 base = d - d % 2 ** (k + 1)
                 carry = jnp.zeros((HP, N), F32)
@@ -322,7 +362,7 @@
                     carry = carry + weight[e, d] * sti[e]
                 zko[k, d] = carry
 
-    for k in range(3):
+    for k in range(1, 3):
 
         @pl.when(bit(z, k))
         def _(k=k):
@@ -334,7 +374,7 @@
 
             @pl.when(bit(peer, k))
             def _():
-                z_send_one(ZKK + k, o, zko.at[k, peer], zkf.at[k, head_rows(z), :]).start()
+                z_send_one(ZKK + k, peer, zko.at[k, peer], zkf.at[k, head_rows(z), :]).start()
 
     def fold(value):
         return sum(value[8 * i : 8 * (i + 1)] for i in range(HP // 8))
@@ -342,6 +382,8 @@
     across = [jnp.zeros((8, N), F32) for _ in range(NZ)]
     for e in range(NZ):
         for d in range(e + 1, NZ + 1):
+            if d < NZ and level_of(e, d) == 0:
+                continue
             other = fsg[...] if d == NZ else dzi[level_of(e, d), d]
             shared = weight[e, d] * fold(sti[e] * other)
             for f in range(e, d):
@@ -353,33 +395,52 @@
     @pl.loop(1, NZ)
     def _(o):
         peer = lax.rem(z + o, NZ)
-        z_send_one(DTT, o, dto.at[peer], dti.at[z]).start()
-
-    @pl.loop(1, NZ)
-    def _(o):
-        peer = lax.rem(z + o, NZ)
-        z_wait(DST, dsf.at[head_rows(peer), :], peer)
+        z_send_one(DTT, peer, dto.at[peer], dti.at[z]).start()
+
+    for p in range(NB):
+
+        @pl.when(jnp.logical_not(bit(z, 0)))
+        def _(p=p):
+            there = low_dz.at[pair_rows(p), :]
+            remote(there, there, n_send.at[0, p], n_recv.at[0, p], at(z + 1, q)).wait_recv()
+
+        @pl.when(bit(z, 0))
+        def _(p=p):
+            low_dz[p * BLK : (p + 1) * BLK, :] = jnp.zeros((BLK, N), F32)
+
+    def upstream_send(p, i):
+        there = up_out.at[:, pl.ds(pl.multiple_of(q * COLS + p * BLK, BLK), BLK)]
+        here = ups.at[i * BLK : (i + 1) * BLK, pair_rows(p)]
+        return remote(here, there, u_send.at[p, i], u_recv.at[p, q], at(z, i, before))
 
     @pl.loop(0, NB)
-    def _(p):
-        cols = pl.ds(pl.multiple_of(p * BLK, BLK), BLK)
-        spread = mm_split(dsf[cols, :], bt16[...])
+    def _(j):
+        p = pair_at(j)
+        cols = pair_rows(p)
+        for half in range(2):
+            owner = 2 * p + half
+
+            @pl.when(owner != z)
+            def _(owner=owner):
+                z_wait(DST, dsf.at[head_rows(owner), :], owner)
+
+        state = dsf[cols, :] + low_dz[cols, :]
+        dsf[cols, :] = state
+        direct = st[cols, :] * low_dz[cols, :]
+        spread = mm_split(state, bt16[...])
         factor = jnp.concatenate(
             [jnp.broadcast_to(f_rows[pl.ds(2 * p + half, 1), :], (HP, TOK)) for half in range(2)], axis=0
         )
         grad = attn[cols, :] + factor * spread
         own = grad * xt[cols, :]
         for half in range(2):
-            xdx[pl.ds(2 * p + half, 1), :] = jnp.sum(own[half * HP : (half + 1) * HP], axis=0, keepdims=True)
+            part = slice(half * HP, (half + 1) * HP)
+            xdx[pl.ds(2 * p + half, 1), :] = jnp.sum(own[part], axis=0, keepdims=True)
+            near[pl.ds(2 * p + half, 1), :] = jnp.sum(direct[part], axis=0, keepdims=True)
         for i in range(NB):
             ups[i * BLK : (i + 1) * BLK, cols] = grad[:, i * BLK : (i + 1) * BLK].T.astype(BF16)
-
-    def up_send(i):
-        there = up_out.at[:, pl.ds(pl.multiple_of(q * COLS, COLS), COLS)]
-        return remote(ups.at[i * BLK : (i + 1) * BLK, :], there, u_send.at[i], u_recv.at[q], at(z, i, before))
-
-    for i in range(NB):
-        up_send(i).start()
+        for i in range(NB):
+            upstream_send(p, i).start()
 
     db_t = jnp.zeros((N, TOK), F32)
     high, low = split(jnp.concatenate([dsf[c * BLK : (c + 1) * BLK, :].T for c in range(NB)], axis=1))
@@ -401,10 +462,16 @@
 
         @pl.when(bit(z, k))
         def _(k=k):
-            @pl.loop(1, NZ)
-            def _(o):
-                peer = lax.rem(z + o, NZ)
-                z_wait(ZKK + k, zkf.at[k, head_rows(peer), :], peer)
+            if k == 0:
+                for p in range(NB):
+                    there = zkf.at[0, pair_rows(p), :]
+                    remote(there, there, n_send.at[1, p], n_recv.at[1, p], at(z - 1, q)).wait_recv()
+            else:
+
+                @pl.loop(1, NZ)
+                def _(o):
+                    peer = lax.rem(z + o, NZ)
+                    z_wait(ZKK + k, zkf.at[k, head_rows(peer), :], peer)
 
             @pl.loop(0, NB)
             def _(p):
@@ -431,9 +498,8 @@
         peer = lax.rem(z + o, NZ)
         z_wait(DTT, dti.at[peer], peer)
 
-    later = jnp.sum(
-        jnp.concatenate([jnp.sum(dti[h], axis=0, keepdims=True) for h in range(HQ)], axis=0), axis=1, keepdims=True
-    )
+    crossing = jnp.concatenate([jnp.sum(dti[h], axis=0, keepdims=True) for h in range(HQ)], axis=0)
+    later = jnp.sum(crossing + near[...], axis=1, keepdims=True)
     pieces = []
     for i in range(NB):
         here = slice(i * BLK, (i + 1) * BLK)
@@ -458,8 +524,8 @@
     for o in range(1, NB):
         rows_send(2, o).start()
         rows_send(3, o).start()
-    own_wg = pltpu.make_async_copy(wgs.at[q], wg_out.at[:, mine, :], loc.at[7])
-    own_dg = pltpu.make_async_copy(dgs.at[q], dg_out.at[mine, :], loc.at[8])
+    own_wg = pltpu.make_async_copy(wgs.at[q], wg_out.at[:, mine, :], loc.at[6, 1])
+    own_dg = pltpu.make_async_copy(dgs.at[q], dg_out.at[mine, :], loc.at[6, 2])
     own_wg.start()
     own_dg.start()
 
@@ -479,36 +545,61 @@
         for kind, there in ((2, wg_out.at[:, theirs, :]), (3, dg_out.at[theirs, :])):
             remote(there, there, o_send.at[kind, o], o_recv.at[kind, peer], at(z, peer)).wait_recv()
     for i in range(NB):
-        there = up_out.at[:, i * COLS : (i + 1) * COLS]
-        remote(there, there, u_send.at[i], u_recv.at[i], at(z, i, before)).wait_recv()
-
-    for kind in range(6):
-        for o in range(1, NB):
-            group_send(kind, o).wait_send()
-    for i in range(NB):
-        up_send(i).wait_send()
+        for p in range(NB):
+            there = up_out.at[:, i * COLS + p * BLK : i * COLS + (p + 1) * BLK]
+            remote(there, there, u_send.at[p, i], u_recv.at[p, i], at(z, i, after)).wait_recv()
+
     for o in range(1, NB):
+        for kind in (DEC, LWT, CPR, BPR):
+            group_send(kind, o, 0).wait_send()
+        for j in range(NB):
+            group_send(GRD, o, j).wait_send()
+            group_send(INP, o, j).wait_send()
         sum_send(0, o).wait_send()
         sum_send(1, o).wait_send()
         rows_send(2, o).wait_send()
         rows_send(3, o).wait_send()
+    for p in range(NB):
+        for i in range(NB):
+            upstream_send(p, i).wait_send()
+
+        @pl.when(bit(z, 0))
+        def _(p=p):
+            down_send(p).wait_send()
+
+        @pl.when(jnp.logical_not(bit(z, 0)))
+        def _(p=p):
+            up_state(p).wait_send()
 
     @pl.loop(1, NZ)
     def _(o):
         peer = lax.rem(z + o, NZ)
-        z_send_one(TOT, o, tot.at[z], tot.at[z]).wait_send()
-        z_send_one(STA, o, st.at[head_rows(peer), :], sti.at[z]).wait_send()
-        z_send_one(DST, o, dso.at[peer], dsf.at[head_rows(z), :]).wait_send()
-        z_send_one(DTT, o, dto.at[peer], dti.at[z]).wait_send()
-        for k in range(3):
+        z_send_one(TOT, peer, tot.at[z], tot.at[z]).wait_send()
+        z_send_one(STA, peer, st.at[head_rows(peer), :], sti.at[z]).wait_send()
+        z_send_one(DST, peer, dso.at[peer], dsf.at[head_rows(z), :]).wait_send()
+        z_send_one(DTT, peer, dto.at[peer], dti.at[z]).wait_send()
+        for k in range(1, 3):
 
             @pl.when(bit(z, k))
             def _(k=k):
-                z_send_one(DZK + k, o, dz.at[k, head_rows(peer), :], dzi.at[k, z]).wait_send()
+                z_send_one(DZK + k, peer, dz.at[k, head_rows(peer), :], dzi.at[k, z]).wait_send()
 
             @pl.when(bit(peer, k))
             def _(k=k):
-                z_send_one(ZKK + k, o, zko.at[k, peer], zkf.at[k, head_rows(z), :]).wait_send()
+                z_send_one(ZKK + k, peer, zko.at[k, peer], zkf.at[k, head_rows(z), :]).wait_send()
+
+
+def hand_over(*refs):
+    sources, targets, held, sem = refs[:5], refs[5:10], refs[10:15], refs[15]
+    taken = [pltpu.make_async_copy(src, mid, sem.at[0, i]) for i, (src, mid) in enumerate(zip(sources, held))]
+    given = [pltpu.make_async_copy(mid, dst, sem.at[1, i]) for i, (mid, dst) in enumerate(zip(held, targets))]
+    for copy in taken:
+        copy.start()
+    for first, second in zip(taken, given):
+        first.wait()
+        second.start()
+    for copy in given:
+        copy.wait()
 
 
 def body(inputs, b_proj, c_proj, decay_log, level_weight, out_grad, final_state_grad):
@@ -559,15 +650,19 @@
         vmem(NB, 6, HQ, BLK),
         vmem(NB, HQ, BLK),
         vmem(HQ, TOK),
-        pltpu.SemaphoreType.DMA((6, NB)),
-        pltpu.SemaphoreType.DMA((6, NB)),
+        vmem(HQ, N),
+        vmem(COLS, N),
+        pltpu.SemaphoreType.DMA((6, NB, NB)),
+        pltpu.SemaphoreType.DMA((6, NB, NB)),
         pltpu.SemaphoreType.DMA((10, NZ)),
         pltpu.SemaphoreType.DMA((10, NZ)),
-        pltpu.SemaphoreType.DMA((NB,)),
-        pltpu.SemaphoreType.DMA((NB,)),
+        pltpu.SemaphoreType.DMA((2, NB)),
+        pltpu.SemaphoreType.DMA((2, NB)),
+        pltpu.SemaphoreType.DMA((NB, NB)),
+        pltpu.SemaphoreType.DMA((NB, NB)),
         pltpu.SemaphoreType.DMA((4, NB)),
         pltpu.SemaphoreType.DMA((4, NB)),
-        pltpu.SemaphoreType.DMA((9,)),
+        pltpu.SemaphoreType.DMA((7, NB)),
     ]
     anywhere = pl.BlockSpec(memory_space=pl.ANY)
     made = (
@@ -577,14 +672,14 @@
         jax.ShapeDtypeStruct((6, HEADS, BLK), F32),
         jax.ShapeDtypeStruct((HEADS, BLK), F32),
     )
-    up, db, dc, wg, dg = pl.pallas_call(
+    results = pl.pallas_call(
         kernel,
         out_shape=made,
         in_specs=[anywhere] * 7,
         out_specs=(anywhere, pl.BlockSpec(memory_space=pltpu.VMEM), pl.BlockSpec(memory_space=pltpu.VMEM), anywhere, anywhere),
         scratch_shapes=scratch,
         compiler_params=pltpu.CompilerParams(
-            collective_id=0, has_side_effects=True, vmem_limit_bytes=40 * 2**20
+            collective_id=0, has_side_effects=True, vmem_limit_bytes=56 * 2**20
         ),
     )(
         inputs[0],
@@ -595,6 +690,14 @@
         jnp.transpose(level_weight[0], (1, 2, 0)),
         jnp.transpose(final_state_grad[0], (0, 2, 1)),
     )
+    up, db, dc, wg, dg = pl.pallas_call(
+        hand_over,
+        out_shape=made,
+        in_specs=[anywhere] * 5,
+        out_specs=[anywhere] * 5,
+        scratch_shapes=[*(pltpu.VMEM(m.shape, m.dtype) for m in made), pltpu.SemaphoreType.DMA((2, 5))],
+        compiler_params=pltpu.CompilerParams(vmem_limit_bytes=56 * 2**20),
+    )(*results)
     return (up[None], db[None], dc[None], dg.T[None], jnp.transpose(wg, (2, 0, 1))[None])
 
 

time: 76.1 us -> 66.5 us (0.87)
  the two profiles are of different devices: /device:TPU:95 before, /device:TPU:1 now
where the time goes in v3:
time: 66.5 us; the launch traced here: 66.4 us
  Pallas kernels  65.7 us (99%)
    pallas_call x1, Pallas kernels, body(): pl.pallas_call(kernel, out_shape=made, in_specs=[anywhere] * 7, out_specs...  63.7 us
    pallas_call x1, Pallas kernels, body(): pl.pallas_call(hand_over, out_shape=made, in_specs=[anywhere] * 5, out_sp...  1.99 us

profile of v3, /device:TPU:1, one launch (start us, length us, event | category | flops | bytes accessed | tf_op | source)
XLA Modules:
  0.0 66.4 jit_solution(12531718607666178910)
XLA Ops:
  0.6 63.7 %shard_map.110 = (bf16[128,2048]{1,0:T(8,128)(2,1)}, f32[128,128]{1,0:T(8,128)}, f32[128,128]{1,0:T(8,128)}, f32[6,32,128]{2,1,0:T(8,128)}, f32[32,128]{1,0:T(8,128)}) custom-call(bf16[128,2048]{1,0:T(8,128)(2,1)} %bitcast.23, bf16[128,2048]{1,0:T(8,128)(2,1)} %bitcast.24, bf16[128,128]{1,0:T(8,128)(2,1)} %bitcast.26, bf16[128,128]{1,0:T(8,128)(2,1)} %bitcast.27, ...), custom_call_target="tpu_custom_call" | custom-call | tf_op jit(solution)/shard_map/pallas_call | solution.py:675
  64.4 2.0 %shard_map.111 = (bf16[128,2048]{1,0:T(8,128)(2,1)}, f32[128,128]{1,0:T(8,128)}, f32[128,128]{1,0:T(8,128)}, f32[6,32,128]{2,1,0:T(8,128)}, f32[32,128]{1,0:T(8,128)}) custom-call(bf16[128,2048]{1,0:T(8,128)(2,1)} %get-tuple-element.15.refs_0_, f32[128,128]{1,0:T(8,128)} %get-tuple-element.16.refs_1_, f32[128,128]{1,0:T(8,128)} %get-tuple-element.17.refs_2_, ...), custom_call_target="tpu_custom_call" | custom-call | tf_op jit(solution)/shard_map/pallas_call | solution.py:693

commit v4 on v3

--- a/solution.py
+++ b/solution.py
@@ -19,7 +19,9 @@
 SECTIONS = 8
 AHEAD = 3
 DEC, LWT, CPR, GRD, BPR, INP = range(6)
-TOT, DZK, STA, DST, ZKK, DTT = 0, 1, 4, 5, 6, 9
+TOT, DZK, JNT, DST, ZKK, DTT = range(6)
+GRAD2, STATE2, STATE3, STATE3_FAR, GRAD3, JOIN3, JOIN3_FAR = range(7)
+TOP = 4
 
 
 def level_of(low, high):
@@ -55,8 +57,9 @@
     xt, gt, gt16, bt16, ct16,
     r_rows, e_rows, f_rows, a_rows, w_rows,
     ag, fx, sp, dp, attn, ups,
-    dz, st, tot, dzi, sti, dso, zko, dto, dsf, zkf, dti,
-    wg, dct, dbs, dcs, dbi, dci, wgs, dgs, xdx, near, low_dz,
+    dz, st, tot, dzi, jnt, dso, zko, dto, dsf, zkf, dti,
+    wg, dct, dbs, dcs, dbi, dci, wgs, dgs, xdx, near,
+    low2, low3, low4, next3, joined, grad3, last, fin,
     a_send, a_recv, z_send, z_recv, n_send, n_recv, u_send, u_recv, o_send, o_recv, loc,
 ):
     seq = lax.axis_index("seq")
@@ -94,8 +97,9 @@
 
     def piece(kind, owner, slot, j):
         heads = pl.ds(pl.multiple_of(owner * HQ, HQ), HQ)
-        there = pl.ds(pl.multiple_of(pair_at(j) * BLK, BLK), BLK)
-        cols = pl.ds(pl.multiple_of(owner * COLS + pair_at(j) * BLK, BLK), BLK)
+        pair = pair_at(j) if kind == GRD else j
+        there = pl.ds(pl.multiple_of(pair * BLK, BLK), BLK)
+        cols = pl.ds(pl.multiple_of(owner * COLS + pair * BLK, BLK), BLK)
         rows = pl.ds(pl.multiple_of(slot * BLK, BLK), BLK)
         if kind == DEC:
             return dec_hbm.at[heads, :], dec.at[slot]
@@ -128,11 +132,11 @@
             dst = piece(kind, peer, peer, j)[1]
             remote(dst, dst, a_send.at[kind, j, o], a_recv.at[kind, j, peer], at(z, peer)).wait_recv()
 
-    for kind in (DEC, LWT, CPR):
+    for kind in (DEC, BPR):
         group_start(kind)
     for j in range(AHEAD):
-        group_start(GRD, j)
-    final_copy = pltpu.make_async_copy(fsg_hbm.at[q * HQ + z], fsg, loc.at[6, 0])
+        group_start(INP, j)
+    final_copy = pltpu.make_async_copy(fsg_hbm.at[pl.ds(pl.multiple_of(q * HQ, HQ), HQ)], fsg, loc.at[6, 0])
     final_copy.start()
 
     row_of = lax.broadcasted_iota(jnp.int32, (BLK, BLK), 0)
@@ -164,6 +168,133 @@
     r_all = r_rows[...]
     e_rows[...] = jnp.exp(r_all)
     f_rows[...] = jnp.exp(sofar - r_all)
+    def bit(zz, k):
+        return lax.rem(zz // 2**k, 2) == 1
+
+    def head_rows(h):
+        return pl.ds(pl.multiple_of(h * HP, HP), HP)
+
+    def pair_rows(p):
+        return pl.ds(pl.multiple_of(p * BLK, BLK), BLK)
+
+    def to_owners(kind, p, source, landing):
+        for half in range(2):
+            owner = 2 * p + half
+
+            @pl.when(owner != z)
+            def _(owner=owner):
+                z_send_one(kind, owner, source.at[head_rows(owner), :], landing.at[z]).start()
+
+            @pl.when(owner == z)
+            def _(owner=owner):
+                landing[z] = source[head_rows(owner), :]
+
+    routes = {
+        STATE2: (st, zkf.at[0], 1),
+        STATE3: (joined.at[0], zkf.at[1], 1),
+        STATE3_FAR: (joined.at[1], zkf.at[1], 2),
+        GRAD2: (dz.at[0], low2, -1),
+        GRAD3: (dz.at[1], next3, -1),
+        JOIN3: (grad3.at[0], low3, -1),
+        JOIN3_FAR: (grad3.at[1], low3, -2),
+    }
+
+    def near_send(kind, p):
+        src, dst, way = routes[kind]
+        rows = pair_rows(p)
+        return remote(src.at[rows, :], dst.at[rows, :], n_send.at[kind, p], n_recv.at[kind, p], at(z + way, q))
+
+    def near_wait(kind, p):
+        _, dst, way = routes[kind]
+        there = dst.at[pair_rows(p), :]
+        remote(there, there, n_send.at[kind, p], n_recv.at[kind, p], at(z - way, q)).wait_recv()
+
+    def per_pair(rows):
+        return jnp.concatenate(
+            [jnp.broadcast_to(rows[half : half + 1], (HP, N)) for half in range(2)], axis=0
+        )
+
+    def total_of(zz, p):
+        return jnp.concatenate([tot[zz, pl.ds(2 * p + half, 1), :] for half in range(2)], axis=0)
+
+    even = jnp.logical_not(bit(z, 0))
+    third = lax.rem(z, 4)
+
+    for k in range(3):
+
+        @pl.when(jnp.logical_not(bit(z, k)))
+        def _(k=k):
+            zkf[k] = jnp.zeros((COLS, N), F32)
+
+    @pl.when(bit(z, 0))
+    def _():
+        low2[...] = jnp.zeros((COLS, N), F32)
+
+    @pl.when(bit(z, 1))
+    def _():
+        low3[...] = jnp.zeros((COLS, N), F32)
+
+    @pl.when(bit(z, 2))
+    def _():
+        low4[...] = jnp.zeros((COLS, N), F32)
+
+    @pl.when(third != 2)
+    def _():
+        next3[...] = jnp.zeros((COLS, N), F32)
+
+    @pl.when(jnp.logical_or(z < TOP, z == NZ - 1))
+    def _():
+        dti[...] = jnp.zeros((NZ, 8, N), F32)
+
+    group_wait(BPR)
+    for i in range(NB):
+        bt16[:, i * BLK : (i + 1) * BLK] = ba[i * BLK : (i + 1) * BLK, :].astype(F32).T.astype(BF16)
+
+    @pl.loop(0, NB)
+    def _(p):
+        cols = pair_rows(p)
+        group_wait(INP, p)
+
+        @pl.when(p < NB - AHEAD)
+        def _():
+            group_start(INP, p + AHEAD)
+            group_start(LWT)
+            group_start(CPR)
+
+        @pl.when(p >= NB - AHEAD)
+        def _():
+            group_start(GRD, p + AHEAD - NB)
+
+        for i in range(NB):
+            xt[cols, i * BLK : (i + 1) * BLK] = xa[i * BLK : (i + 1) * BLK, cols].astype(F32).T
+        for half in range(2):
+            rows = head_rows(2 * p + half)
+            high, low = split(xt[rows, :] * f_rows[pl.ds(2 * p + half, 1), :])
+            fx[0, rows, :] = high
+            fx[1, rows, :] = low
+        st[cols, :] = mm(fx[0, cols, :], ba[...]) + mm(fx[1, cols, :], ba[...])
+
+        @pl.when(even)
+        def _():
+            near_send(STATE2, p).start()
+
+    @pl.loop(1, NZ)
+    def _(o):
+        peer = lax.rem(z + o, NZ)
+        z_wait(TOT, tot.at[peer], peer)
+
+    @pl.when(third == 1)
+    def _():
+        @pl.loop(0, NB)
+        def _(p):
+            rows = pair_rows(p)
+            near_wait(STATE2, p)
+            both = per_pair(jnp.exp(total_of(z, p))) * zkf[0, rows, :] + st[rows, :]
+            joined[0, rows, :] = both
+            joined[1, rows, :] = per_pair(jnp.exp(total_of(z + 1, p))) * both
+            near_send(STATE3, p).start()
+            near_send(STATE3_FAR, p).start()
+
     group_wait(LWT)
     for k in range(3):
         for i in range(NB):
@@ -179,33 +310,6 @@
     dct[...] = jnp.zeros_like(dct)
     dp[...] = jnp.zeros_like(dp)
 
-    def bit(zz, k):
-        return lax.rem(zz // 2**k, 2) == 1
-
-    def head_rows(h):
-        return pl.ds(pl.multiple_of(h * HP, HP), HP)
-
-    def pair_rows(p):
-        return pl.ds(pl.multiple_of(p * BLK, BLK), BLK)
-
-    def to_owners(kind, p, source, landing):
-        for half in range(2):
-            owner = 2 * p + half
-
-            @pl.when(owner != z)
-            def _(owner=owner):
-                z_send_one(kind, owner, source.at[head_rows(owner), :], landing.at[z]).start()
-
-            @pl.when(owner == z)
-            def _(owner=owner):
-                landing[z] = source[head_rows(owner), :]
-
-    def down_send(p):
-        return remote(dz.at[0, pair_rows(p), :], low_dz.at[pair_rows(p), :], n_send.at[0, p], n_recv.at[0, p], at(z - 1, q))
-
-    def up_state(p):
-        return remote(st.at[pair_rows(p), :], zkf.at[0, pair_rows(p), :], n_send.at[1, p], n_recv.at[1, p], at(z + 1, q))
-
     @pl.loop(0, NB)
     def _(j):
         p = pair_at(j)
@@ -216,19 +320,11 @@
         def _():
             group_start(GRD, j + AHEAD)
 
-        @pl.when(j == NB - AHEAD)
-        def _():
-            group_start(BPR)
-
-        @pl.when(j >= NB - AHEAD)
-        def _():
-            group_start(INP, j + AHEAD - NB)
-
         for i in range(NB):
             rows = ga[i * BLK : (i + 1) * BLK, cols].astype(F32).T
             gt[cols, i * BLK : (i + 1) * BLK] = rows
             gt16[cols, i * BLK : (i + 1) * BLK] = rows.astype(BF16)
-        for k in range(3):
+        for k in (2, 1, 0):
 
             @pl.when(bit(z, k))
             def _(k=k):
@@ -238,78 +334,38 @@
                     ag[k, 0, rows, :] = high
                     ag[k, 1, rows, :] = low
                 dz[k, cols, :] = mm(ag[k, 0, cols, :], ca[...]) + mm(ag[k, 1, cols, :], ca[...])
-                if k == 0:
-                    down_send(p).start()
+                if k == 2:
+                    to_owners(DZK, p, dz.at[k], dzi)
+                elif k == 1:
+
+                    @pl.when(third == 3)
+                    def _():
+                        near_send(GRAD3, p).start()
                 else:
-                    to_owners(DZK + k, p, dz.at[k], dzi.at[k])
-
-    group_wait(BPR)
-    for i in range(NB):
-        bt16[:, i * BLK : (i + 1) * BLK] = ba[i * BLK : (i + 1) * BLK, :].astype(F32).T.astype(BF16)
-
-    @pl.loop(0, NB)
-    def _(j):
-        p = pair_at(j)
-        cols = pair_rows(p)
-        group_wait(INP, j)
-
-        @pl.when(j == 0)
-        def _():
-            group_start(INP, NB - 1)
-
-        for i in range(NB):
-            xt[cols, i * BLK : (i + 1) * BLK] = xa[i * BLK : (i + 1) * BLK, cols].astype(F32).T
-        for half in range(2):
-            rows = head_rows(2 * p + half)
-            high, low = split(xt[rows, :] * f_rows[pl.ds(2 * p + half, 1), :])
-            fx[0, rows, :] = high
-            fx[1, rows, :] = low
-        st[cols, :] = mm(fx[0, cols, :], ba[...]) + mm(fx[1, cols, :], ba[...])
-
-        @pl.when(jnp.logical_not(bit(z, 0)))
-        def _():
-            up_state(p).start()
-
-        to_owners(STA, p, st, sti)
-
-    @pl.loop(1, NZ)
-    def _(o):
-        peer = lax.rem(z + o, NZ)
-        z_wait(TOT, tot.at[peer], peer)
-
-    for k in range(1, 3):
-
-        @pl.loop(1, NZ)
-        def _(o, k=k):
-            peer = lax.rem(z + o, NZ)
-
-            @pl.when(bit(peer, k))
-            def _():
-                z_wait(DZK + k, dzi.at[k, peer], peer)
-
-    final_copy.wait()
-    totals = [tot[d, pl.ds(z, 1), :] for d in range(NZ)]
-    weight = {}
-    for e in range(NZ):
-        gap = jnp.zeros((1, BLK), F32)
-        for d in range(e + 1, NZ):
-            weight[e, d] = jnp.exp(gap)
-            gap = gap + totals[d]
-        weight[e, NZ] = jnp.exp(gap)
-    for e in range(NZ):
-        grad = weight[e, NZ] * fsg[...]
-        for d in range(e + 1, NZ):
-            if level_of(e, d) == 0:
-                continue
-            grad = grad + weight[e, d] * dzi[level_of(e, d), d]
-        dso[e] = grad
-
-    dsf[head_rows(z), :] = dso[z]
-
-    @pl.loop(1, NZ)
-    def _(o):
-        peer = lax.rem(z + o, NZ)
-        z_send_one(DST, peer, dso.at[peer], dsf.at[head_rows(z), :]).start()
+                    near_send(GRAD2, p).start()
+
+    @pl.when(z == TOP - 1)
+    def _():
+        @pl.loop(0, NB)
+        def _(p):
+            rows = pair_rows(p)
+            near_wait(STATE2, p)
+            near_wait(STATE3_FAR, p)
+            carried = zkf[0, rows, :] + zkf[1, rows, :]
+            joined[0, rows, :] = per_pair(jnp.exp(total_of(z, p))) * carried + st[rows, :]
+            to_owners(JNT, p, joined.at[0], jnt)
+
+    @pl.when(third == 2)
+    def _():
+        @pl.loop(0, NB)
+        def _(p):
+            rows = pair_rows(p)
+            near_wait(GRAD3, p)
+            both = dz[1, rows, :] + per_pair(jnp.exp(total_of(z, p))) * next3[rows, :]
+            grad3[0, rows, :] = both
+            grad3[1, rows, :] = per_pair(jnp.exp(total_of(z - 1, p))) * both
+            near_send(JOIN3, p).start()
+            near_send(JOIN3_FAR, p).start()
 
     sp[...] = mm(ba[...], ct16[...])
 
@@ -348,65 +404,69 @@
                 row = jnp.concatenate([found[half][level, j] for j in range(NB)], axis=1)
                 wg[level, pl.ds(2 * p + half, 1), :] = row
 
-    @pl.loop(1, NZ)
-    def _(o):
-        peer = lax.rem(z + o, NZ)
-        z_wait(STA, sti.at[peer], peer)
-
-    for d in range(1, NZ):
-        for k in range(1, 3):
-            if d >> k & 1:
-                base = d - d % 2 ** (k + 1)
-                carry = jnp.zeros((HP, N), F32)
-                for e in range(base, base + 2**k):
-                    carry = carry + weight[e, d] * sti[e]
-                zko[k, d] = carry
-
-    for k in range(1, 3):
-
-        @pl.when(bit(z, k))
-        def _(k=k):
-            zkf[k, head_rows(z), :] = zko[k, z]
-
-        @pl.loop(1, NZ)
-        def _(o, k=k):
-            peer = lax.rem(z + o, NZ)
-
-            @pl.when(bit(peer, k))
-            def _():
-                z_send_one(ZKK + k, peer, zko.at[k, peer], zkf.at[k, head_rows(z), :]).start()
+    for d in range(TOP, NZ):
+
+        @pl.when(z != d)
+        def _(d=d):
+            z_wait(DZK, dzi.at[d], d)
+
+    totals = [tot[d, pl.ds(z, 1), :] for d in range(NZ)]
+    upto_here = {TOP: jnp.zeros((1, N), F32)}
+    for d in range(TOP + 1, NZ):
+        upto_here[d] = upto_here[d - 1] + totals[d - 1]
+    reach4 = {d: jnp.exp(gap) for d, gap in upto_here.items()}
+    joint_grad = dzi[TOP]
+    for d in range(TOP + 1, NZ):
+        joint_grad = joint_grad + reach4[d] * dzi[d]
+    gap = jnp.zeros((1, N), F32)
+    for e in reversed(range(TOP)):
+        dso[e] = jnp.exp(gap) * joint_grad
+        gap = gap + totals[e]
+
+        @pl.when(z != e)
+        def _(e=e):
+            z_send_one(DST, e, dso.at[e], low4.at[head_rows(z), :]).start()
+
+        @pl.when(z == e)
+        def _(e=e):
+            low4[head_rows(z), :] = dso[e]
+
+    @pl.when(z != TOP - 1)
+    def _():
+        z_wait(JNT, jnt.at[TOP - 1], TOP - 1)
+
+    for d in range(TOP, NZ):
+        zko[d] = reach4[d] * jnt[TOP - 1]
+
+        @pl.when(z != d)
+        def _(d=d):
+            z_send_one(ZKK, d, zko.at[d], zkf.at[2, head_rows(z), :]).start()
+
+        @pl.when(z == d)
+        def _(d=d):
+            zkf[2, head_rows(z), :] = zko[d]
 
     def fold(value):
         return sum(value[8 * i : 8 * (i + 1)] for i in range(HP // 8))
 
-    across = [jnp.zeros((8, N), F32) for _ in range(NZ)]
-    for e in range(NZ):
-        for d in range(e + 1, NZ + 1):
-            if d < NZ and level_of(e, d) == 0:
-                continue
-            other = fsg[...] if d == NZ else dzi[level_of(e, d), d]
-            shared = weight[e, d] * fold(sti[e] * other)
-            for f in range(e, d):
-                across[f] = across[f] + shared
-    for f in range(NZ):
-        dto[f] = across[f]
-    dti[z] = dto[z]
-
-    @pl.loop(1, NZ)
-    def _(o):
-        peer = lax.rem(z + o, NZ)
-        z_send_one(DTT, peer, dto.at[peer], dti.at[z]).start()
-
-    for p in range(NB):
-
-        @pl.when(jnp.logical_not(bit(z, 0)))
-        def _(p=p):
-            there = low_dz.at[pair_rows(p), :]
-            remote(there, there, n_send.at[0, p], n_recv.at[0, p], at(z + 1, q)).wait_recv()
-
-        @pl.when(bit(z, 0))
-        def _(p=p):
-            low_dz[p * BLK : (p + 1) * BLK, :] = jnp.zeros((BLK, N), F32)
+    across = jnp.zeros((8, N), F32)
+    for f in reversed(range(TOP, NZ - 1)):
+        across = across + fold(zko[f + 1] * dzi[f + 1])
+        dto[f] = across
+
+        @pl.when(z != f)
+        def _(f=f):
+            z_send_one(DTT, f, dto.at[f], dti.at[z]).start()
+
+        @pl.when(z == f)
+        def _(f=f):
+            dti[z] = dto[f]
+
+    final_copy.wait()
+    rest = jnp.zeros((HQ, N), F32)
+    for f in range(1, NZ):
+        rest = rest + tot[f] * jnp.where(z < f, 1.0, 0.0)
+    fin[...] = jnp.exp(rest)
 
     def upstream_send(p, i):
         there = up_out.at[:, pl.ds(pl.multiple_of(q * COLS + p * BLK, BLK), BLK)]
@@ -417,16 +477,31 @@
     def _(j):
         p = pair_at(j)
         cols = pair_rows(p)
+
+        @pl.when(even)
+        def _():
+            near_wait(GRAD2, p)
+
+        @pl.when(third == 1)
+        def _():
+            near_wait(JOIN3, p)
+
+        @pl.when(third == 0)
+        def _():
+            near_wait(JOIN3_FAR, p)
+
         for half in range(2):
             owner = 2 * p + half
 
-            @pl.when(owner != z)
+            @pl.when(jnp.logical_and(z < TOP, owner != z))
             def _(owner=owner):
-                z_wait(DST, dsf.at[head_rows(owner), :], owner)
-
-        state = dsf[cols, :] + low_dz[cols, :]
+                z_wait(DST, low4.at[head_rows(owner), :], owner)
+
+        weight = jnp.concatenate([fin[pl.ds(2 * p + half, 1), :] for half in range(2)], axis=0)
+        ending = per_pair(weight) * fsg[pl.ds(2 * p, 2)].reshape(BLK, N)
+        last[cols, :] = ending
+        state = ending + low2[cols, :] + low3[cols, :] + low4[cols, :]
         dsf[cols, :] = state
-        direct = st[cols, :] * low_dz[cols, :]
         spread = mm_split(state, bt16[...])
         factor = jnp.concatenate(
             [jnp.broadcast_to(f_rows[pl.ds(2 * p + half, 1), :], (HP, TOK)) for half in range(2)], axis=0
@@ -436,7 +511,6 @@
         for half in range(2):
             part = slice(half * HP, (half + 1) * HP)
             xdx[pl.ds(2 * p + half, 1), :] = jnp.sum(own[part], axis=0, keepdims=True)
-            near[pl.ds(2 * p + half, 1), :] = jnp.sum(direct[part], axis=0, keepdims=True)
         for i in range(NB):
             ups[i * BLK : (i + 1) * BLK, cols] = grad[:, i * BLK : (i + 1) * BLK].T.astype(BF16)
         for i in range(NB):
@@ -463,15 +537,28 @@
         @pl.when(bit(z, k))
         def _(k=k):
             if k == 0:
-                for p in range(NB):
-                    there = zkf.at[0, pair_rows(p), :]
-                    remote(there, there, n_send.at[1, p], n_recv.at[1, p], at(z - 1, q)).wait_recv()
+
+                @pl.when(z == NZ - 1)
+                def _():
+                    for p in range(NB):
+                        near_wait(STATE2, p)
+            elif k == 1:
+
+                @pl.when(third == 2)
+                def _():
+                    for p in range(NB):
+                        near_wait(STATE3, p)
+
+                @pl.when(z == NZ - 1)
+                def _():
+                    for p in range(NB):
+                        near_wait(STATE3_FAR, p)
             else:
 
                 @pl.loop(1, NZ)
                 def _(o):
                     peer = lax.rem(z + o, NZ)
-                    z_wait(ZKK + k, zkf.at[k, head_rows(peer), :], peer)
+                    z_wait(ZKK, zkf.at[2, head_rows(peer), :], peer)
 
             @pl.loop(0, NB)
             def _(p):
@@ -493,10 +580,23 @@
         sum_send(1, o).start()
     dci[q] = dcs[q]
 
-    @pl.loop(1, NZ)
-    def _(o):
-        peer = lax.rem(z + o, NZ)
-        z_wait(DTT, dti.at[peer], peer)
+    @pl.when(jnp.logical_and(z >= TOP, z < NZ - 1))
+    def _():
+        @pl.loop(1, NZ)
+        def _(o):
+            peer = lax.rem(z + o, NZ)
+            z_wait(DTT, dti.at[peer], peer)
+
+    @pl.loop(0, NB)
+    def _(p):
+        rows = pair_rows(p)
+        lower = zkf[0, rows, :] + zkf[1, rows, :]
+        carried = zkf[1, rows, :] * next3[rows, :] + zkf[0, rows, :] * low3[rows, :]
+        carried = carried + lower * low4[rows, :] + (lower + zkf[2, rows, :]) * last[rows, :]
+        own = st[rows, :] * dsf[rows, :] + per_pair(jnp.exp(total_of(z, p))) * carried
+        for half in range(2):
+            part = slice(half * HP, (half + 1) * HP)
+            near[pl.ds(2 * p + half, 1), :] = jnp.sum(own[part], axis=0, keepdims=True)
 
     crossing = jnp.concatenate([jnp.sum(dti[h], axis=0, keepdims=True) for h in range(HQ)], axis=0)
     later = jnp.sum(crossing + near[...], axis=1, keepdims=True)
@@ -563,30 +663,52 @@
         for i in range(NB):
             upstream_send(p, i).wait_send()
 
+        @pl.when(even)
+        def _(p=p):
+            near_send(STATE2, p).wait_send()
+
         @pl.when(bit(z, 0))
         def _(p=p):
-            down_send(p).wait_send()
-
-        @pl.when(jnp.logical_not(bit(z, 0)))
+            near_send(GRAD2, p).wait_send()
+
+        @pl.when(third == 1)
         def _(p=p):
-            up_state(p).wait_send()
+            near_send(STATE3, p).wait_send()
+            near_send(STATE3_FAR, p).wait_send()
+
+        @pl.when(third == 2)
+        def _(p=p):
+            near_send(JOIN3, p).wait_send()
+            near_send(JOIN3_FAR, p).wait_send()
+
+        @pl.when(third == 3)
+        def _(p=p):
+            near_send(GRAD3, p).wait_send()
 
     @pl.loop(1, NZ)
     def _(o):
         peer = lax.rem(z + o, NZ)
         z_send_one(TOT, peer, tot.at[z], tot.at[z]).wait_send()
-        z_send_one(STA, peer, st.at[head_rows(peer), :], sti.at[z]).wait_send()
-        z_send_one(DST, peer, dso.at[peer], dsf.at[head_rows(z), :]).wait_send()
-        z_send_one(DTT, peer, dto.at[peer], dti.at[z]).wait_send()
-        for k in range(1, 3):
-
-            @pl.when(bit(z, k))
-            def _(k=k):
-                z_send_one(DZK + k, peer, dz.at[k, head_rows(peer), :], dzi.at[k, z]).wait_send()
-
-            @pl.when(bit(peer, k))
-            def _(k=k):
-                z_send_one(ZKK + k, peer, zko.at[k, peer], zkf.at[k, head_rows(z), :]).wait_send()
+
+        @pl.when(z >= TOP)
+        def _():
+            z_send_one(DZK, peer, dz.at[2, head_rows(peer), :], dzi.at[z]).wait_send()
+
+        @pl.when(z == TOP - 1)
+        def _():
+            z_send_one(JNT, peer, joined.at[0, head_rows(peer), :], jnt.at[z]).wait_send()
+
+        @pl.when(peer < TOP)
+        def _():
+            z_send_one(DST, peer, dso.at[peer], low4.at[head_rows(z), :]).wait_send()
+
+        @pl.when(peer >= TOP)
+        def _():
+            z_send_one(ZKK, peer, zko.at[peer], zkf.at[2, head_rows(z), :]).wait_send()
+
+        @pl.when(jnp.logical_and(peer >= TOP, peer < NZ - 1))
+        def _():
+            z_send_one(DTT, peer, dto.at[peer], dti.at[z]).wait_send()
 
 
 def hand_over(*refs):
@@ -613,7 +735,7 @@
         vmem(TOK, N, dtype=BF16),
         vmem(NB, HQ, BLK),
         vmem(NB, 6, HQ, BLK),
-        vmem(HP, N),
+        vmem(HQ, HP, N),
         vmem(COLS, TOK),
         vmem(COLS, TOK),
         vmem(COLS, TOK, dtype=BF16),
@@ -633,10 +755,10 @@
         vmem(3, COLS, N),
         vmem(COLS, N),
         vmem(NZ, HQ, BLK),
-        vmem(3, NZ, HP, N),
         vmem(NZ, HP, N),
         vmem(NZ, HP, N),
-        vmem(3, NZ, HP, N),
+        vmem(NZ, HP, N),
+        vmem(NZ, HP, N),
         vmem(NZ, 8, N),
         vmem(COLS, N),
         vmem(3, COLS, N),
@@ -652,12 +774,19 @@
         vmem(HQ, TOK),
         vmem(HQ, N),
         vmem(COLS, N),
+        vmem(COLS, N),
+        vmem(COLS, N),
+        vmem(COLS, N),
+        vmem(2, COLS, N),
+        vmem(2, COLS, N),
+        vmem(COLS, N),
+        vmem(HQ, N),
         pltpu.SemaphoreType.DMA((6, NB, NB)),
         pltpu.SemaphoreType.DMA((6, NB, NB)),
-        pltpu.SemaphoreType.DMA((10, NZ)),
-        pltpu.SemaphoreType.DMA((10, NZ)),
-        pltpu.SemaphoreType.DMA((2, NB)),
-        pltpu.SemaphoreType.DMA((2, NB)),
+        pltpu.SemaphoreType.DMA((6, NZ)),
+        pltpu.SemaphoreType.DMA((6, NZ)),
+        pltpu.SemaphoreType.DMA((7, NB)),
+        pltpu.SemaphoreType.DMA((7, NB)),
         pltpu.SemaphoreType.DMA((NB, NB)),
         pltpu.SemaphoreType.DMA((NB, NB)),
         pltpu.SemaphoreType.DMA((4, NB)),

time: 66.5 us -> 78.7 us (1.18)
  Pallas kernels: 65.7 us -> 78 us
    pallas_call x1, Pallas kernels: 63.7 us -> 76 us  [body(): pl.pallas_call(kernel, out_shape=made, in_specs=[anywhere] * 7, out_specs...]
where the time goes in v4:
time: 78.7 us; the launch traced here: 78.6 us
  Pallas kernels  78 us (99%)
    pallas_call x1, Pallas kernels, body(): pl.pallas_call(kernel, out_shape=made, in_specs=[anywhere] * 7, out_specs...  76 us
    pallas_call x1, Pallas kernels, body(): pl.pallas_call(hand_over, out_shape=made, in_specs=[anywhere] * 5, out_sp...  1.99 us

profile of v4, /device:TPU:1, one launch (start us, length us, event | category | flops | bytes accessed | tf_op | source)
XLA Modules:
  0.0 78.6 jit_solution(1654060397616899651)
XLA Ops:
  0.6 76.0 %shard_map.110 = (bf16[128,2048]{1,0:T(8,128)(2,1)}, f32[128,128]{1,0:T(8,128)}, f32[128,128]{1,0:T(8,128)}, f32[6,32,128]{2,1,0:T(8,128)}, f32[32,128]{1,0:T(8,128)}) custom-call(bf16[128,2048]{1,0:T(8,128)(2,1)} %bitcast.23, bf16[128,2048]{1,0:T(8,128)(2,1)} %bitcast.24, bf16[128,128]{1,0:T(8,128)(2,1)} %bitcast.26, bf16[128,128]{1,0:T(8,128)(2,1)} %bitcast.27, ...), custom_call_target="tpu_custom_call" | custom-call | tf_op jit(solution)/shard_map/pallas_call | solution.py:804
  76.6 2.0 %shard_map.111 = (bf16[128,2048]{1,0:T(8,128)(2,1)}, f32[128,128]{1,0:T(8,128)}, f32[128,128]{1,0:T(8,128)}, f32[6,32,128]{2,1,0:T(8,128)}, f32[32,128]{1,0:T(8,128)}) custom-call(bf16[128,2048]{1,0:T(8,128)(2,1)} %get-tuple-element.15.refs_0_, f32[128,128]{1,0:T(8,128)} %get-tuple-element.16.refs_1_, f32[128,128]{1,0:T(8,128)} %get-tuple-element.17.refs_2_, ...), custom_call_target="tpu_custom_call" | custom-call | tf_op jit(solution)/shard_map/pallas_call | solution.py:822

commit v5 on v3

--- a/solution.py
+++ b/solution.py
@@ -17,7 +17,8 @@
 TOK = NB * BLK
 COLS = HQ * HP
 SECTIONS = 8
-AHEAD = 3
+AHEAD = 4
+FED = 6
 DEC, LWT, CPR, GRD, BPR, INP = range(6)
 TOT, DZK, STA, DST, ZKK, DTT = 0, 1, 4, 5, 6, 9
 
@@ -56,7 +57,7 @@
     r_rows, e_rows, f_rows, a_rows, w_rows,
     ag, fx, sp, dp, attn, ups,
     dz, st, tot, dzi, sti, dso, zko, dto, dsf, zkf, dti,
-    wg, dct, dbs, dcs, dbi, dci, wgs, dgs, xdx, near, low_dz,
+    wg, dct, dbs, dcs, dbi, dci, wgs, dgs, xdx, near, low_dz, last, fin,
     a_send, a_recv, z_send, z_recv, n_send, n_recv, u_send, u_recv, o_send, o_recv, loc,
 ):
     seq = lax.axis_index("seq")
@@ -132,7 +133,7 @@
         group_start(kind)
     for j in range(AHEAD):
         group_start(GRD, j)
-    final_copy = pltpu.make_async_copy(fsg_hbm.at[q * HQ + z], fsg, loc.at[6, 0])
+    final_copy = pltpu.make_async_copy(fsg_hbm.at[pl.ds(pl.multiple_of(q * HQ, HQ), HQ)], fsg, loc.at[6, 0])
     final_copy.start()
 
     row_of = lax.broadcasted_iota(jnp.int32, (BLK, BLK), 0)
@@ -176,7 +177,6 @@
     for i in range(NB):
         ct16[:, i * BLK : (i + 1) * BLK] = ca[i * BLK : (i + 1) * BLK, :].astype(F32).T.astype(BF16)
     wg[...] = jnp.zeros_like(wg)
-    dct[...] = jnp.zeros_like(dct)
     dp[...] = jnp.zeros_like(dp)
 
     def bit(zz, k):
@@ -205,6 +205,16 @@
 
     def up_state(p):
         return remote(st.at[pair_rows(p), :], zkf.at[0, pair_rows(p), :], n_send.at[1, p], n_recv.at[1, p], at(z + 1, q))
+
+    for k in range(3):
+
+        @pl.when(jnp.logical_not(bit(z, k)))
+        def _(k=k):
+            zkf[k] = jnp.zeros((COLS, N), F32)
+
+    @pl.when(z >= FED)
+    def _():
+        dsf[...] = jnp.zeros((COLS, N), F32)
 
     @pl.loop(0, NB)
     def _(j):
@@ -253,9 +263,9 @@
         cols = pair_rows(p)
         group_wait(INP, j)
 
-        @pl.when(j == 0)
-        def _():
-            group_start(INP, NB - 1)
+        @pl.when(j < NB - AHEAD)
+        def _():
+            group_start(INP, j + AHEAD)
 
         for i in range(NB):
             xt[cols, i * BLK : (i + 1) * BLK] = xa[i * BLK : (i + 1) * BLK, cols].astype(F32).T
@@ -270,46 +280,9 @@
         def _():
             up_state(p).start()
 
-        to_owners(STA, p, st, sti)
-
-    @pl.loop(1, NZ)
-    def _(o):
-        peer = lax.rem(z + o, NZ)
-        z_wait(TOT, tot.at[peer], peer)
-
-    for k in range(1, 3):
-
-        @pl.loop(1, NZ)
-        def _(o, k=k):
-            peer = lax.rem(z + o, NZ)
-
-            @pl.when(bit(peer, k))
-            def _():
-                z_wait(DZK + k, dzi.at[k, peer], peer)
-
-    final_copy.wait()
-    totals = [tot[d, pl.ds(z, 1), :] for d in range(NZ)]
-    weight = {}
-    for e in range(NZ):
-        gap = jnp.zeros((1, BLK), F32)
-        for d in range(e + 1, NZ):
-            weight[e, d] = jnp.exp(gap)
-            gap = gap + totals[d]
-        weight[e, NZ] = jnp.exp(gap)
-    for e in range(NZ):
-        grad = weight[e, NZ] * fsg[...]
-        for d in range(e + 1, NZ):
-            if level_of(e, d) == 0:
-                continue
-            grad = grad + weight[e, d] * dzi[level_of(e, d), d]
-        dso[e] = grad
-
-    dsf[head_rows(z), :] = dso[z]
-
-    @pl.loop(1, NZ)
-    def _(o):
-        peer = lax.rem(z + o, NZ)
-        z_send_one(DST, peer, dso.at[peer], dsf.at[head_rows(z), :]).start()
+        @pl.when(z < FED)
+        def _():
+            to_owners(STA, p, st, sti)
 
     sp[...] = mm(ba[...], ct16[...])
 
@@ -348,10 +321,59 @@
                 row = jnp.concatenate([found[half][level, j] for j in range(NB)], axis=1)
                 wg[level, pl.ds(2 * p + half, 1), :] = row
 
+    high, low = split(dp[...])
+    dct[...] = mm(bt16[...], high) + mm(bt16[...], low)
+    for i in range(NB):
+        dbs[i] = mm_split(dp[i * BLK : (i + 1) * BLK, :], ca[...])
+
     @pl.loop(1, NZ)
     def _(o):
         peer = lax.rem(z + o, NZ)
-        z_wait(STA, sti.at[peer], peer)
+        z_wait(TOT, tot.at[peer], peer)
+
+    for k in range(1, 3):
+
+        @pl.loop(1, NZ)
+        def _(o, k=k):
+            peer = lax.rem(z + o, NZ)
+
+            @pl.when(bit(peer, k))
+            def _():
+                z_wait(DZK + k, dzi.at[k, peer], peer)
+
+    totals = [tot[d, pl.ds(z, 1), :] for d in range(NZ)]
+    weight = {}
+    for e in range(FED):
+        gap = jnp.zeros((1, BLK), F32)
+        for d in range(e + 1, NZ):
+            weight[e, d] = jnp.exp(gap)
+            gap = gap + totals[d]
+    for e in range(FED):
+        grad = jnp.zeros((HP, N), F32)
+        for d in range(e + 1, NZ):
+            if level_of(e, d) > 0:
+                grad = grad + weight[e, d] * dzi[level_of(e, d), d]
+        dso[e] = grad
+
+    @pl.when(z < FED)
+    def _():
+        dsf[head_rows(z), :] = dso[z]
+
+    @pl.loop(1, NZ)
+    def _(o):
+        peer = lax.rem(z + o, NZ)
+
+        @pl.when(peer < FED)
+        def _():
+            z_send_one(DST, peer, dso.at[peer], dsf.at[head_rows(z), :]).start()
+
+    @pl.loop(1, NZ)
+    def _(o):
+        peer = lax.rem(z + o, NZ)
+
+        @pl.when(peer < FED)
+        def _():
+            z_wait(STA, sti.at[peer], peer)
 
     for d in range(1, NZ):
         for k in range(1, 3):
@@ -380,12 +402,11 @@
         return sum(value[8 * i : 8 * (i + 1)] for i in range(HP // 8))
 
     across = [jnp.zeros((8, N), F32) for _ in range(NZ)]
-    for e in range(NZ):
-        for d in range(e + 1, NZ + 1):
-            if d < NZ and level_of(e, d) == 0:
+    for e in range(FED):
+        for d in range(e + 1, NZ):
+            if level_of(e, d) == 0:
                 continue
-            other = fsg[...] if d == NZ else dzi[level_of(e, d), d]
-            shared = weight[e, d] * fold(sti[e] * other)
+            shared = weight[e, d] * fold(sti[e] * dzi[level_of(e, d), d])
             for f in range(e, d):
                 across[f] = across[f] + shared
     for f in range(NZ):
@@ -397,6 +418,32 @@
         peer = lax.rem(z + o, NZ)
         z_send_one(DTT, peer, dto.at[peer], dti.at[z]).start()
 
+    def carried_level(k):
+        @pl.when(bit(z, k))
+        def _():
+            if k == 0:
+                for p in range(NB):
+                    there = zkf.at[0, pair_rows(p), :]
+                    remote(there, there, n_send.at[1, p], n_recv.at[1, p], at(z - 1, q)).wait_recv()
+            else:
+
+                @pl.loop(1, NZ)
+                def _(o):
+                    peer = lax.rem(z + o, NZ)
+                    z_wait(ZKK + k, zkf.at[k, head_rows(peer), :], peer)
+
+            @pl.loop(0, NB)
+            def _(p):
+                cols = pl.ds(pl.multiple_of(p * BLK, BLK), BLK)
+                reach = mm_split(zkf[k, cols, :], ct16[...]) * gt[cols, :]
+                for half in range(2):
+                    h = 2 * p + half
+                    row = jnp.sum(reach[half * HP : (half + 1) * HP], axis=0, keepdims=True)
+                    wg[3 + k, pl.ds(h, 1), :] = row * e_rows[pl.ds(h, 1), :]
+
+            high, low = split(jnp.concatenate([zkf[k, c * BLK : (c + 1) * BLK, :].T for c in range(NB)], axis=1))
+            dct[...] += mm(high, ag[k, 0]) + mm(low, ag[k, 0]) + mm(high, ag[k, 1])
+
     for p in range(NB):
 
         @pl.when(jnp.logical_not(bit(z, 0)))
@@ -407,6 +454,15 @@
         @pl.when(bit(z, 0))
         def _(p=p):
             low_dz[p * BLK : (p + 1) * BLK, :] = jnp.zeros((BLK, N), F32)
+
+    def per_pair(rows):
+        return jnp.concatenate([jnp.broadcast_to(row, (HP, N)) for row in rows], axis=0)
+
+    final_copy.wait()
+    rest = jnp.zeros((HQ, N), F32)
+    for f in range(1, NZ):
+        rest = rest + tot[f] * jnp.where(z < f, 1.0, 0.0)
+    fin[...] = jnp.exp(rest)
 
     def upstream_send(p, i):
         there = up_out.at[:, pl.ds(pl.multiple_of(q * COLS + p * BLK, BLK), BLK)]
@@ -420,13 +476,15 @@
         for half in range(2):
             owner = 2 * p + half
 
-            @pl.when(owner != z)
+            @pl.when(jnp.logical_and(z < FED, owner != z))
             def _(owner=owner):
                 z_wait(DST, dsf.at[head_rows(owner), :], owner)
 
-        state = dsf[cols, :] + low_dz[cols, :]
+        ending = per_pair([fin[pl.ds(2 * p + half, 1), :] for half in range(2)])
+        ending = ending * fsg[pl.ds(2 * p, 2)].reshape(BLK, N)
+        last[cols, :] = ending
+        state = dsf[cols, :] + low_dz[cols, :] + ending
         dsf[cols, :] = state
-        direct = st[cols, :] * low_dz[cols, :]
         spread = mm_split(state, bt16[...])
         factor = jnp.concatenate(
             [jnp.broadcast_to(f_rows[pl.ds(2 * p + half, 1), :], (HP, TOK)) for half in range(2)], axis=0
@@ -436,18 +494,19 @@
         for half in range(2):
             part = slice(half * HP, (half + 1) * HP)
             xdx[pl.ds(2 * p + half, 1), :] = jnp.sum(own[part], axis=0, keepdims=True)
-            near[pl.ds(2 * p + half, 1), :] = jnp.sum(direct[part], axis=0, keepdims=True)
         for i in range(NB):
             ups[i * BLK : (i + 1) * BLK, cols] = grad[:, i * BLK : (i + 1) * BLK].T.astype(BF16)
         for i in range(NB):
             upstream_send(p, i).start()
 
+    carried_level(0)
+
     db_t = jnp.zeros((N, TOK), F32)
     high, low = split(jnp.concatenate([dsf[c * BLK : (c + 1) * BLK, :].T for c in range(NB)], axis=1))
     db_t = mm(high, fx[0]) + mm(low, fx[0]) + mm(high, fx[1])
     for i in range(NB):
         keys = slice(i * BLK, (i + 1) * BLK)
-        dbs[i] = mm_split(dp[keys, :], ca[...]) + db_t[:, keys].T
+        dbs[i] += db_t[:, keys].T
 
     def sum_send(kind, o):
         peer = lax.rem(q + o, NB)
@@ -458,35 +517,10 @@
         sum_send(0, o).start()
     dbi[q] = dbs[q]
 
-    for k in range(3):
-
-        @pl.when(bit(z, k))
-        def _(k=k):
-            if k == 0:
-                for p in range(NB):
-                    there = zkf.at[0, pair_rows(p), :]
-                    remote(there, there, n_send.at[1, p], n_recv.at[1, p], at(z - 1, q)).wait_recv()
-            else:
-
-                @pl.loop(1, NZ)
-                def _(o):
-                    peer = lax.rem(z + o, NZ)
-                    z_wait(ZKK + k, zkf.at[k, head_rows(peer), :], peer)
-
-            @pl.loop(0, NB)
-            def _(p):
-                cols = pl.ds(pl.multiple_of(p * BLK, BLK), BLK)
-                reach = mm_split(zkf[k, cols, :], ct16[...]) * gt[cols, :]
-                for half in range(2):
-                    h = 2 * p + half
-                    row = jnp.sum(reach[half * HP : (half + 1) * HP], axis=0, keepdims=True)
-                    wg[3 + k, pl.ds(h, 1), :] = row * e_rows[pl.ds(h, 1), :]
-
-            high, low = split(jnp.concatenate([zkf[k, c * BLK : (c + 1) * BLK, :].T for c in range(NB)], axis=1))
-            dct[...] += mm(high, ag[k, 0]) + mm(low, ag[k, 0]) + mm(high, ag[k, 1])
-
-    high, low = split(dp[...])
-    dc_t = dct[...] + mm(bt16[...], high) + mm(bt16[...], low)
+    for k in (1, 2):
+        carried_level(k)
+
+    dc_t = dct[...]
     for i in range(NB):
         dcs[i] = dc_t[:, i * BLK : (i + 1) * BLK].T
     for o in range(1, NB):
@@ -497,6 +531,16 @@
     def _(o):
         peer = lax.rem(z + o, NZ)
         z_wait(DTT, dti.at[peer], peer)
+
+    @pl.loop(0, NB)
+    def _(p):
+        rows = pair_rows(p)
+        decay = per_pair([jnp.exp(tot[z, pl.ds(2 * p + half, 1), :]) for half in range(2)])
+        ended = decay * (zkf[0, rows, :] + zkf[1, rows, :] + zkf[2, rows, :]) + st[rows, :]
+        own = st[rows, :] * low_dz[rows, :] + ended * last[rows, :]
+        for half in range(2):
+            part = slice(half * HP, (half + 1) * HP)
+            near[pl.ds(2 * p + half, 1), :] = jnp.sum(own[part], axis=0, keepdims=True)
 
     crossing = jnp.concatenate([jnp.sum(dti[h], axis=0, keepdims=True) for h in range(HQ)], axis=0)
     later = jnp.sum(crossing + near[...], axis=1, keepdims=True)
@@ -575,8 +619,15 @@
     def _(o):
         peer = lax.rem(z + o, NZ)
         z_send_one(TOT, peer, tot.at[z], tot.at[z]).wait_send()
-        z_send_one(STA, peer, st.at[head_rows(peer), :], sti.at[z]).wait_send()
-        z_send_one(DST, peer, dso.at[peer], dsf.at[head_rows(z), :]).wait_send()
+
+        @pl.when(z < FED)
+        def _():
+            z_send_one(STA, peer, st.at[head_rows(peer), :], sti.at[z]).wait_send()
+
+        @pl.when(peer < FED)
+        def _():
+            z_send_one(DST, peer, dso.at[peer], dsf.at[head_rows(z), :]).wait_send()
+
         z_send_one(DTT, peer, dto.at[peer], dti.at[z]).wait_send()
         for k in range(1, 3):
 
@@ -613,7 +664,7 @@
         vmem(TOK, N, dtype=BF16),
         vmem(NB, HQ, BLK),
         vmem(NB, 6, HQ, BLK),
-        vmem(HP, N),
+        vmem(HQ, HP, N),
         vmem(COLS, TOK),
         vmem(COLS, TOK),
         vmem(COLS, TOK, dtype=BF16),
@@ -652,6 +703,8 @@
         vmem(HQ, TOK),
         vmem(HQ, N),
         vmem(COLS, N),
+        vmem(COLS, N),
+        vmem(HQ, N),
         pltpu.SemaphoreType.DMA((6, NB, NB)),
         pltpu.SemaphoreType.DMA((6, NB, NB)),
         pltpu.SemaphoreType.DMA((10, NZ)),

time: 66.5 us -> 63.1 us (0.949)
  Pallas kernels: 65.7 us -> 62.3 us
    pallas_call x1, Pallas kernels: 63.7 us -> 60.3 us  [body(): pl.pallas_call(kernel, out_shape=made, in_specs=[anywhere] * 7, out_specs...]
where the time goes in v5:
time: 63.1 us; the launch traced here: 63 us
  Pallas kernels  62.3 us (99%)
  between operations  0.64 us (1%)
    pallas_call x1, Pallas kernels, body(): pl.pallas_call(kernel, out_shape=made, in_specs=[anywhere] * 7, out_specs...  60.3 us
    pallas_call x1, Pallas kernels, body(): pl.pallas_call(hand_over, out_shape=made, in_specs=[anywhere] * 5, out_sp...  1.99 us

profile of v5, /device:TPU:1, one launch (start us, length us, event | category | flops | bytes accessed | tf_op | source)
XLA Modules:
  0.0 63.0 jit_solution(13611978437369077429)
XLA Ops:
  0.6 60.3 %shard_map.110 = (bf16[128,2048]{1,0:T(8,128)(2,1)}, f32[128,128]{1,0:T(8,128)}, f32[128,128]{1,0:T(8,128)}, f32[6,32,128]{2,1,0:T(8,128)}, f32[32,128]{1,0:T(8,128)}) custom-call(bf16[128,2048]{1,0:T(8,128)(2,1)} %bitcast.23, bf16[128,2048]{1,0:T(8,128)(2,1)} %bitcast.24, bf16[128,128]{1,0:T(8,128)(2,1)} %bitcast.26, bf16[128,128]{1,0:T(8,128)(2,1)} %bitcast.27, ...), custom_call_target="tpu_custom_call" | custom-call | tf_op jit(solution)/shard_map/pallas_call | solution.py:728
  61.0 2.0 %shard_map.111 = (bf16[128,2048]{1,0:T(8,128)(2,1)}, f32[128,128]{1,0:T(8,128)}, f32[128,128]{1,0:T(8,128)}, f32[6,32,128]{2,1,0:T(8,128)}, f32[32,128]{1,0:T(8,128)}) custom-call(bf16[128,2048]{1,0:T(8,128)(2,1)} %get-tuple-element.15.refs_0_, f32[128,128]{1,0:T(8,128)} %get-tuple-element.16.refs_1_, f32[128,128]{1,0:T(8,128)} %get-tuple-element.17.refs_2_, ...), custom_call_target="tpu_custom_call" | custom-call | tf_op jit(solution)/shard_map/pallas_call | solution.py:746

commit v6 on v5

--- a/solution.py
+++ b/solution.py
@@ -57,7 +57,7 @@
     r_rows, e_rows, f_rows, a_rows, w_rows,
     ag, fx, sp, dp, attn, ups,
     dz, st, tot, dzi, sti, dso, zko, dto, dsf, zkf, dti,
-    wg, dct, dbs, dcs, dbi, dci, wgs, dgs, xdx, near, low_dz, last, fin,
+    wg, dct, dbs, dcs, dbi, dci, wgs, dgs, xdx, near, low_dz, last, fin, summed,
     a_send, a_recv, z_send, z_recv, n_send, n_recv, u_send, u_recv, o_send, o_recv, loc,
 ):
     seq = lax.axis_index("seq")
@@ -578,11 +578,13 @@
             peer = lax.rem(q + o, NB)
             there = landed.at[peer]
             remote(there, there, o_send.at[kind, o], o_recv.at[kind, peer], at(z, peer)).wait_recv()
-    db_out[...] = dbi[0] + dbi[1] + dbi[2] + dbi[3]
-    dc_out[...] = dci[0] + dci[1] + dci[2] + dci[3]
+        summed[kind] = landed[0] + landed[1] + landed[2] + landed[3]
+        pltpu.make_async_copy(summed.at[kind], (db_out, dc_out)[kind], loc.at[7, kind]).start()
 
     own_wg.wait()
     own_dg.wait()
+    late_db = pltpu.make_async_copy(summed.at[0], db_out, loc.at[7, 0])
+    late_dc = pltpu.make_async_copy(summed.at[1], dc_out, loc.at[7, 1])
     for o in range(1, NB):
         peer = lax.rem(q + o, NB)
         theirs = pl.ds(pl.multiple_of(peer * HQ, HQ), HQ)
@@ -592,6 +594,9 @@
         for p in range(NB):
             there = up_out.at[:, i * COLS + p * BLK : i * COLS + (p + 1) * BLK]
             remote(there, there, u_send.at[p, i], u_recv.at[p, i], at(z, i, after)).wait_recv()
+
+    late_db.wait()
+    late_dc.wait()
 
     for o in range(1, NB):
         for kind in (DEC, LWT, CPR, BPR):
@@ -705,6 +710,7 @@
         vmem(COLS, N),
         vmem(COLS, N),
         vmem(HQ, N),
+        vmem(2, BLK, N),
         pltpu.SemaphoreType.DMA((6, NB, NB)),
         pltpu.SemaphoreType.DMA((6, NB, NB)),
         pltpu.SemaphoreType.DMA((10, NZ)),
@@ -715,7 +721,7 @@
         pltpu.SemaphoreType.DMA((NB, NB)),
         pltpu.SemaphoreType.DMA((4, NB)),
         pltpu.SemaphoreType.DMA((4, NB)),
-        pltpu.SemaphoreType.DMA((7, NB)),
+        pltpu.SemaphoreType.DMA((8, NB)),
     ]
     anywhere = pl.BlockSpec(memory_space=pl.ANY)
     made = (
@@ -729,7 +735,7 @@
         kernel,
         out_shape=made,
         in_specs=[anywhere] * 7,
-        out_specs=(anywhere, pl.BlockSpec(memory_space=pltpu.VMEM), pl.BlockSpec(memory_space=pltpu.VMEM), anywhere, anywhere),
+        out_specs=[anywhere] * 5,
         scratch_shapes=scratch,
         compiler_params=pltpu.CompilerParams(
             collective_id=0, has_side_effects=True, vmem_limit_bytes=56 * 2**20

time: 63.1 us -> 62.5 us (level)
  no operation moved by 1% of the time
where the time goes in v6:
time: 62.5 us; the launch traced here: 62.3 us
  Pallas kernels  61.7 us (99%)
  between operations  0.64 us (1%)
    pallas_call x1, Pallas kernels, body(): pl.pallas_call(kernel, out_shape=made, in_specs=[anywhere] * 7, out_specs...  59.7 us
    pallas_call x1, Pallas kernels, body(): pl.pallas_call(hand_over, out_shape=made, in_specs=[anywhere] * 5, out_sp...  1.99 us

profile of v6, /device:TPU:1, one launch (start us, length us, event | category | flops | bytes accessed | tf_op | source)
XLA Modules:
  0.0 62.3 jit_solution(14328121103065426084)
XLA Ops:
  0.6 59.7 %shard_map.110 = (bf16[128,2048]{1,0:T(8,128)(2,1)}, f32[128,128]{1,0:T(8,128)}, f32[128,128]{1,0:T(8,128)}, f32[6,32,128]{2,1,0:T(8,128)}, f32[32,128]{1,0:T(8,128)}) custom-call(bf16[128,2048]{1,0:T(8,128)(2,1)} %bitcast.23, bf16[128,2048]{1,0:T(8,128)(2,1)} %bitcast.24, bf16[128,128]{1,0:T(8,128)(2,1)} %bitcast.26, bf16[128,128]{1,0:T(8,128)(2,1)} %bitcast.27, ...), custom_call_target="tpu_custom_call" | custom-call | tf_op jit(solution)/shard_map/pallas_call | solution.py:734
  60.4 2.0 %shard_map.111 = (bf16[128,2048]{1,0:T(8,128)(2,1)}, f32[128,128]{1,0:T(8,128)}, f32[128,128]{1,0:T(8,128)}, f32[6,32,128]{2,1,0:T(8,128)}, f32[32,128]{1,0:T(8,128)}) custom-call(bf16[128,2048]{1,0:T(8,128)(2,1)} %get-tuple-element.15.refs_0_, f32[128,128]{1,0:T(8,128)} %get-tuple-element.16.refs_1_, f32[128,128]{1,0:T(8,128)} %get-tuple-element.17.refs_2_, ...), custom_call_target="tpu_custom_call" | custom-call | tf_op jit(solution)/shard_map/pallas_call | solution.py:752
